TPU v7x, 256 devices: a whole 4x4x8 slice. The times are simulated.
256 devices in a mesh: dp: 16 (over z_hi, x, core), cell: 16 (over z_lo, y).
Axes of the slice: x: 4, y: 4, z: 8 (z_hi: 2, z_lo: 4; z = z_hi * 4 + z_lo), core: 2. Of those that a mesh axis runs over, the one named last changes fastest.
Arguments:
- jacobian: float32 [1024, 64, 64, 32], P('dp', 'cell'), may hold values from -0.03314563 to 0.03314563
- smooth_x: float32 [4, 64, 64], replicated, may hold values from 0 to 1.5, as said below
- smooth_y: float32 [4, 64, 64], replicated, may hold values from 0 to 1.5, as said below
- smooth_z: float32 [4, 32, 32], replicated, may hold values from 0 to 1.5, as said below
- index_x: int32 [64, 32], replicated, may hold values from 0 to 3
- index_y: int32 [64, 32], P('cell'), may hold values from 0 to 3
- index_z: int32 [64, 64], P('cell'), may hold values from 0 to 3
Outputs:
- normal_matrix: float32 [1024, 1024], P('dp', 'cell')
Inputs may be any that keep to these rules, and one draw needn't show every extreme that they name: `smooth_x`: zero where the two indices differ by more than 3; nonnegative. `smooth_y`: zero where the two indices differ by more than 3; nonnegative. `smooth_z`: zero where the two indices differ by more than 3; nonnegative.
All inputs are finite; a program needn't handle non-finite values.
Results may differ from a plain program's by a relative error of at most 0.003.
Values may be sent and summed in bfloat16 or wider, within the bound.
No kernel may reach another device: no remote copies, remote signals or barrier semaphores. Data moves between devices by JAX's collectives and lax.ppermute only.
A program may use at most 64 MiB of HBM per device.

v0:
```python
import jax
import jax.numpy as jnp
from jax import lax
from jax.sharding import PartitionSpec as P

BAND = 3


def for_sending(array):

    def short(part):
        return part.astype(jnp.bfloat16) if part.dtype == jnp.float32 else part

    return jax.tree.map(short, array)


def band_rows(tables):
    padded = jnp.pad(tables, ((0, 0), (0, 0), (BAND, BAND)))
    return jnp.stack(
        [
            jnp.diagonal(padded, offset=shift_no, axis1=1, axis2=2)
            for shift_no in range(2 * BAND + 1)
        ],
        0,
    )


def pick_bands(bands, labels):
    picked = jnp.zeros((bands.shape[0],) + labels.shape + (bands.shape[2],), jnp.float32)
    for table_no in range(bands.shape[1]):
        chosen = (labels == table_no)[None, ..., None]
        picked = picked + jnp.where(
            chosen, bands[:, table_no][(slice(None),) + (None,) * labels.ndim], jnp.float32(0.0)
        )
    return picked


def banded_apply(coefs, extended, axis_no, length):
    running = coefs[0][None] * lax.slice_in_dim(extended, 0, length, axis=axis_no)
    for shift_no in range(1, coefs.shape[0]):
        running = running + coefs[shift_no][None] * lax.slice_in_dim(
            extended, shift_no, shift_no + length, axis=axis_no
        )
    return running


def pad_axis(operand, axis_no):
    widths = [(0, 0)] * operand.ndim
    widths[axis_no] = (BAND, BAND)
    return jnp.pad(operand, widths)


def inner_rows(left_side, right_side):
    return lax.dot_general(
        left_side, right_side, (((1,), (1,)), ((), ())), preferred_element_type=jnp.float32
    )


def body(jacobian, smooth_x, smooth_y, smooth_z, index_x, index_y, index_z):
    row_count, slab_width, width_y, width_z = jacobian.shape
    coef_z = pick_bands(band_rows(smooth_z), index_z)
    along_z = banded_apply(coef_z, pad_axis(jacobian, 3), 3, width_z)
    coef_y = jnp.swapaxes(pick_bands(band_rows(smooth_y), index_y), 2, 3)
    along_y = banded_apply(coef_y, pad_axis(along_z, 2), 2, width_y)
    bands_x = band_rows(smooth_x)
    gathered = lax.all_to_all(
        for_sending(along_y.reshape(row_count, slab_width, width_y * width_z)),
        "cell",
        split_axis=2,
        concat_axis=1,
        tiled=True,
    )
    group_width = gathered.shape[2]
    labels = lax.dynamic_slice_in_dim(
        index_x.reshape(-1), lax.axis_index("cell") * group_width, group_width, 0
    )
    coef_x = jnp.swapaxes(pick_bands(bands_x, labels), 1, 2)
    smoothed = banded_apply(coef_x, pad_axis(gathered, 1), 1, gathered.shape[1])
    returned = lax.all_to_all(
        for_sending(smoothed), "cell", split_axis=1, concat_axis=2, tiled=True
    ).astype(smoothed.dtype)
    flat_cells = returned.reshape(row_count, -1)
    panel_rows = flat_cells.astype(jnp.bfloat16)
    partial_value = inner_rows(panel_rows, lax.all_gather(panel_rows, "dp", axis=0, tiled=True))
    return lax.psum_scatter(partial_value, "cell", scatter_dimension=1, tiled=True)


def solution(mesh):
    return jax.shard_map(
        body,
        mesh=mesh,
        in_specs=(
            P("dp", "cell", None, None),
            P(),
            P(),
            P(),
            P(),
            P("cell", None),
            P("cell", None),
        ),
        out_specs=P("dp", "cell"),
        check_vma=False,
    )
```

profile of v0, /device:TPU:8, one launch (start us, length us, event | category | flops | bytes accessed | tf_op | source)
XLA Modules:
  0.0 399.9 jit_solution(4375721691630574761)
XLA Ops:
  15.4 2.7 copy.120
  18.2 1.6 pad.24
  22.7 1.5 gather_fusion.18
  24.2 1.5 gather_fusion.17
  25.7 1.5 gather_fusion.16
  28.7 1.5 gather_fusion.1
  31.1 13.5 %fusion.6 = f32[64,4,64,32]{2,3,1,0:T(8,128)S(1)} fusion(f32[64,4,64,32]{2,3,1,0:T(8,128)} %param.13, f32[4,64,32]{1,2,0:T(8,128)S(1)} %get-tuple-element.29, f32[4,64,32]{1,2,0:T(8,128)S(1)} %get-tuple-element.30, f32[4,64,32]{1,2,0:T(8,128)S(1)} %get-tuple-element.31, f32[4,64,32]{1,2,0:T(8,128)S(1)} %get-tuple-element.32, ...), kind=kLoop, calls=%fused_computation.33 | loop fusion | flops 6815744 | bytes 4423680 | tf_op jit(solution)/shard_map/add | solution.py:41
  44.6 6.6 %add_convert_fusion = bf16[64,4,64,32]{2,3,1,0:T(8,128)(2,1)S(1)} fusion(f32[64,4,64,32]{2,3,1,0:T(8,128)S(1)} %fusion.6, f32[4,64,32]{1,2,0:T(8,128)S(1)} %get-tuple-element.22, f32[4,64,32]{1,2,0:T(8,128)S(1)} %get-tuple-element.23, f32[4,64,32]{1,2,0:T(8,128)S(1)} %get-tuple-element.24, f32[4,64,32]{1,2,0:T(8,128)S(1)} %get-tuple-element.25, ...), kind=kLoop, calls=%fused_computation.39 | loop fusion | flops 7340032 | bytes 3375104 | tf_op jit(solution)/shard_map/convert_element_type | solution.py:12
  51.2 4.9 %copy.129 = bf16[64,4,64,32]{0,3,2,1:T(8,128)(2,1)} copy(bf16[64,4,64,32]{2,3,1,0:T(8,128)(2,1)S(1)} %add_convert_fusion) | data formatting | bytes 2097152 | tf_op jit(solution)/shard_map/convert_element_type | solution.py:12
  56.2 3.5 copy.151
  59.6 2.3 reshape.428
  61.9 9.1 %all-to-all-start = ((bf16[16,2,16384]{2,1,0:T(2,128)(2,1)}), bf16[16,2,16384]{2,1,0:T(2,128)(2,1)S(1)}, u32[]{:S(2)}, u32[]{:S(2)}) async-start(bf16[16,2,16384]{2,1,0:T(2,128)(2,1)} %reshape.428), calls=%async_computation | async-start | bytes 2097152 | tf_op jit(solution)/shard_map/all_to_all | solution.py:66
  71.3 1.8 copy.119
  73.2 1.6 pad.23
  76.3 1.5 gather_fusion
  82.5 1.5 gather_fusion.11
  84.0 1.5 gather_fusion.10
  86.5 7.5 %all-to-all-done = bf16[16,2,16384]{2,1,0:T(2,128)(2,1)S(1)} async-done(((bf16[16,2,16384]{2,1,0:T(2,128)(2,1)}), bf16[16,2,16384]{2,1,0:T(2,128)(2,1)S(1)}, u32[]{:S(2)}, u32[]{:S(2)}) %all-to-all-start) | async-done | bytes 1048608 | tf_op jit(solution)/shard_map/all_to_all | solution.py:66
  96.4 2.2 add_convert_fusion.1
  98.7 31.8 %all_to_all.36 = bf16[64,64,128]{2,0,1:T(8,128)(2,1)S(1)} all-to-all(bf16[64,64,128]{2,0,1:T(8,128)(2,1)S(1)} %add_convert_fusion.1), channel_id=1, replica_groups=mesh['dp'=16,'cell'=16] {'cell'}, dimensions={1} | all-to-all | bytes 2097152 | tf_op jit(solution)/shard_map/all_to_all | solution.py:79
  131.1 1.7 copy.150
  132.9 174.9 %all-gather.2.cloned.1.call-done = bf16[1024,8192]{1,0:T(8,128)(2,1)} async-done(((bf16[64,8192]{1,0:T(8,128)(2,1)}), bf16[1024,8192]{1,0:T(8,128)(2,1)}) %all-gather.2.cloned.1.call-update) | async-done | bytes 16777232 | tf_op jit(solution)/shard_map/all_gather | solution.py:84
  307.8 9.4 %convolution_bitcast_fusion = f32[1024,64]{1,0:T(8,128)} fusion(bf16[1024,8192]{1,0:T(8,128)(2,1)} %all-gather.2.cloned.1.call-done, bf16[8,8,64,128]{3,2,1,0:T(8,128)(2,1)S(1)} %bitcast.185), kind=kOutput, calls=%fused_computation.46 | convolution fusion | flops 1073741824 | bytes 18087936
  317.2 74.4 %reduce-scatter.4.cloned.1.call-done = f32[64,64]{1,0:T(8,128)} async-done(((f32[1024,64]{1,0:T(8,128)}), f32[64,64]{1,0:T(8,128)}) %reduce-scatter.4.cloned.1.call-update) | async-done | bytes 16400
  (87 shorter events, 25.9 us)
Async XLA Ops:
  56.2 15.2 %copy-start = (f32[4,64,64]{2,1,0:T(8,128)S(1)}, f32[4,64,64]{2,1,0:T(8,128)}, u32[]{:S(2)}) copy-start(f32[4,64,64]{2,1,0:T(8,128)} %param.14) | copy-start | bytes 196612
  61.9 15.9 %copy-start.1 = (s32[64,32]{0,1:T(8,128)S(1)}, s32[64,32]{0,1:T(8,128)}, u32[]{:S(2)}) copy-start(s32[64,32]{0,1:T(8,128)} %param.17) | copy-start | bytes 24580
  61.9 32.1 %all-to-all-start = ((bf16[16,2,16384]{2,1,0:T(2,128)(2,1)}), bf16[16,2,16384]{2,1,0:T(2,128)(2,1)S(1)}, u32[]{:S(2)}, u32[]{:S(2)}) async-start(bf16[16,2,16384]{2,1,0:T(2,128)(2,1)} %reshape.428), calls=%async_computation | async-start | bytes 2097152 | tf_op jit(solution)/shard_map/all_to_all | solution.py:66
  71.1 236.8 %all-gather.2.cloned.1.call-start = ((), (), s32[]{:S(2)}) async-start(), calls=%async_computation.3 | async-start | bytes 17825792 | tf_op jit(solution)/shard_map/all_gather | solution.py:84
  132.9 258.8 %reduce-scatter.4.cloned.1.call-start = ((), (), s32[]{:S(2)}) async-start(), calls=%async_computation.4 | async-start | bytes 557056
Sparse Core Ops, SparseCore 0:
  133.0 174.8 all-gather.1
  317.4 74.2 reduce-scatter.3
where the time goes:
time: 405 us; the launch traced here: 400 us
  waiting for transfers between devices  257 us (63%)
  local copies, waits for them, and re-layouts  54.1 us (13%)
  blocking collectives  31.8 us (8%)
  other arithmetic  24.6 us (6%)
  between operations  13.8 us (3%)
  starting transfers between devices  9.42 us (2%)
  matrix products  9.38 us (2%)
    all_gather x1, waiting for transfers between devices, body(): lax.all_gather(panel_rows, 'dp', axis=0, tiled=True)  175 us
    unnamed x3, waiting for transfers between devices  74.4 us
    all_to_all x1, blocking collectives, body(): lax.all_to_all(for_sending(smoothed), 'cell', split_axis=1, concat_axis=2...  31.8 us
    gather x28, local copies, waits for them, and re-layouts, band_rows(): jnp.diagonal(padded, offset=shift_no, axis1=1, axis2=2)  26.5 us
    add x1, other arithmetic, banded_apply(): running + coefs[shift_no][None] * lax.slice_in_dim(extended, shift_no, sh...  13.5 us
    unnamed x32, local copies, waits for them, and re-layouts  12.9 us
    unnamed x1, matrix products  9.38 us
    all_to_all x1, starting transfers between devices, body(): lax.all_to_all(for_sending(along_y.reshape(row_count, slab_width, width_y...  9.12 us
  transfers between devices with their start and end apart: 3, of which 3 were waited for; matrix products, arithmetic and copies ran while one was open for 4% of the time, Pallas kernels for 0%

commit v1 on v0

v1 whole, which is shorter than its diff:
```python
import functools

import jax
import jax.numpy as jnp
from jax import lax
from jax.experimental import pallas as pl
from jax.experimental.pallas import tpu as pltpu
from jax.sharding import Mesh, PartitionSpec as P

BAND = 3
TAPS = 2 * BAND + 1
TABLES = 4
F32 = jnp.float32
BF16 = jnp.bfloat16
VMEM = pl.BlockSpec(memory_space=pltpu.VMEM)
SMEM = pl.BlockSpec(memory_space=pltpu.SMEM)


def split_table(table):
    high = table.astype(BF16)
    low = (table - high.astype(F32)).astype(BF16)
    return high, low


def band_column(table, tap):
    rows = lax.broadcasted_iota(jnp.int32, table.shape, 0)
    cols = lax.broadcasted_iota(jnp.int32, table.shape, 1)
    return jnp.sum(jnp.where(cols == rows + (tap - BAND), table, 0.0), axis=1, keepdims=True)


def zy_kernel(index_y, index_z, table_y, table_z, jac, out, coef):
    group = pl.program_id(0)
    rows, planes, nz, ny = jac.shape
    lhs = []
    for t in range(TABLES):
        high, low = split_table(table_y[t])
        lhs.append(jnp.concatenate([high, low], axis=1))
    lhs = jnp.concatenate(lhs, axis=0)
    for tap in range(TAPS):
        cols = [band_column(table_z[t], tap) for t in range(TABLES)]
        for x in range(planes):
            label = index_z[pl.ds(group * planes + x, 1), :]
            picked = jnp.broadcast_to(cols[0], (nz, ny))
            for t in range(1, TABLES):
                picked = jnp.where(label == t, cols[t], picked)
            coef[x, tap] = picked
    lane = lax.broadcasted_iota(jnp.int32, (1, planes * rows), 1)
    for z in range(0, nz, 2):
        parts = []
        for zz in (z, z + 1):
            for x in range(planes):
                total = None
                for tap in range(TAPS):
                    w = zz + tap - BAND
                    if 0 <= w < nz:
                        term = coef[x, tap, pl.ds(zz, 1), :] * jac[:, x, w, :]
                        total = term if total is None else total + term
                short = total.astype(BF16)
                parts.append(jnp.concatenate([short, short], axis=1))
        rhs = jnp.concatenate(parts, axis=0)
        both = lax.dot_general(lhs, rhs, (((1,), (1,)), ((), ())), preferred_element_type=F32)
        for k, zz in enumerate((z, z + 1)):
            label = jnp.full_like(lane, index_y[group * planes, zz])
            for x in range(1, planes):
                label = jnp.where(lane >= x * rows, index_y[group * planes + x, zz], label)
            part = both[:, k * planes * rows : (k + 1) * planes * rows]
            picked = part[:ny]
            for t in range(1, TABLES):
                picked = jnp.where(label == t, part[t * ny : (t + 1) * ny], picked)
            out[zz] = picked.astype(BF16)


def smooth_zy(jacobian, smooth_y, smooth_z, index_y, index_z):
    rows, slab, ny, nz = jacobian.shape
    planes = 2
    return pl.pallas_call(
        zy_kernel,
        grid=(slab // planes,),
        out_shape=jax.ShapeDtypeStruct((nz, ny, slab * rows), BF16),
        in_specs=[
            SMEM,
            VMEM,
            VMEM,
            VMEM,
            pl.BlockSpec((rows, planes, nz, ny), lambda i: (0, i, 0, 0)),
        ],
        out_specs=pl.BlockSpec((nz, ny, planes * rows), lambda i: (0, 0, i)),
        scratch_shapes=[pltpu.VMEM((planes, TAPS, nz, ny), F32)],
        compiler_params=pltpu.CompilerParams(vmem_limit_bytes=40 * 2**20),
        name="smooth_zy",
    )(index_y, index_z, smooth_y, smooth_z, jnp.swapaxes(jacobian, 2, 3))


def x_kernel(place, index_x, table_x, got, out, wide, bands):
    z, y0 = place[0], place[1]
    columns = got.shape[1]
    cells, per = 16, 4
    nx = cells * per
    for t in range(TABLES):
        table = table_x[t]
        for tap in range(TAPS):
            bands[t, tap] = jnp.broadcast_to(band_column(table, tap), (nx, 128))
    row = index_x[pl.ds(z, 1), :]
    sub = lax.broadcasted_iota(jnp.int32, (columns, row.shape[1]), 0)
    lan = lax.broadcasted_iota(jnp.int32, (columns, row.shape[1]), 1)
    label = jnp.sum(jnp.where(lan == sub + y0, row, 0).astype(F32), axis=1, keepdims=True)
    label = jnp.broadcast_to(label, (columns, 128))
    left = lax.broadcasted_iota(jnp.int32, (columns, 128), 1) < 64

    for edge in range(BAND):
        wide[edge] = jnp.zeros(wide.shape[1:], F32)
        wide[nx + BAND + edge] = jnp.zeros(wide.shape[1:], F32)

    @pl.loop(0, cells)
    def _(cell):
        for parity in range(2):
            for zh in range(2):
                first = (zh * 4 + parity) * cells + cell
                second = (zh * 4 + 2 + parity) * cells + cell
                lanes = pl.ds((parity * 2 + zh) * 128, 128)
                for pair in range(per // 2):
                    a = got[first, :, pl.ds(pair * 128, 128)].astype(F32)
                    b = got[second, :, pl.ds(pair * 128, 128)].astype(F32)
                    base = cell * per + pair * 2 + BAND
                    wide[base, :, lanes] = jnp.where(left, a, pltpu.roll(b, 64, 1))
                    wide[base + 1, :, lanes] = jnp.where(left, pltpu.roll(a, 64, 1), b)

    @pl.loop(0, nx)
    def _(x):
        totals = [None] * 4
        for tap in range(TAPS):
            coef = jnp.broadcast_to(bands[0, tap, pl.ds(x, 1), :], label.shape)
            for t in range(1, TABLES):
                coef = jnp.where(label == t, bands[t, tap, pl.ds(x, 1), :], coef)
            for block in range(4):
                term = coef * wide[x + tap, :, pl.ds(block * 128, 128)]
                totals[block] = term if tap == 0 else totals[block] + term
        for block in range(4):
            out[x, :, pl.ds(block * 128, 128)] = totals[block].astype(BF16)


def smooth_x_local(got, smooth_x, index_x, place):
    columns = got.shape[1]
    nx = smooth_x.shape[1]
    return pl.pallas_call(
        x_kernel,
        out_shape=jax.ShapeDtypeStruct((nx, columns, 512), BF16),
        in_specs=[SMEM, VMEM, VMEM, VMEM],
        out_specs=VMEM,
        scratch_shapes=[
            pltpu.VMEM((nx + 2 * BAND, columns, 512), F32),
            pltpu.VMEM((TABLES, TAPS, nx, 128), F32),
        ],
        compiler_params=pltpu.CompilerParams(vmem_limit_bytes=40 * 2**20),
        name="smooth_x",
    )(place, jnp.swapaxes(index_x, 0, 1), smooth_x, got)


def gram_kernel(core, own, other, out):
    mine = core[0]
    left = own[...]
    for k, right in enumerate((own, other)):
        which = mine if k == 0 else 1 - mine
        for part in range(2):
            piece = lax.dot_general(
                left,
                right[:, part * 256 : (part + 1) * 256],
                (((0,), (0,)), ((), ())),
                preferred_element_type=F32,
            ).astype(BF16)
            for x in range(4):
                for zh in range(2):
                    start = ((x % 2 * 2 + zh) * 2 + x // 2) * 64
                    out[x, part * 2 + which, pl.ds(zh * 64, 64), :] = piece[start : start + 64]


def gram(core, own, other):
    return pl.pallas_call(
        gram_kernel,
        out_shape=jax.ShapeDtypeStruct((4, 4, 128, 256), BF16),
        in_specs=[SMEM, VMEM, VMEM],
        out_specs=VMEM,
        compiler_params=pltpu.CompilerParams(vmem_limit_bytes=40 * 2**20),
        name="gram",
    )(core, own, other)


def sum_plane_kernel(got, out):
    total = got[0].astype(F32)
    for k in range(1, got.shape[0]):
        total = total + got[k].astype(F32)
    for zh in range(2):
        for zl in range(4):
            block = total[zh * 64 : (zh + 1) * 64, zl * 64 : (zl + 1) * 64]
            out[zh * 4 + zl] = jnp.concatenate([block[:32], block[32:]], axis=1)


def sum_plane(got):
    return pl.pallas_call(
        sum_plane_kernel,
        out_shape=jax.ShapeDtypeStruct((8, 32, 128), F32),
        in_specs=[VMEM],
        out_specs=VMEM,
        name="sum_plane",
    )(got)


def sum_line_kernel(got, out):
    total = got[0]
    for k in range(1, got.shape[0]):
        total = total + got[k]
    out[pl.ds(0, 32), :] = total[:, :64]
    out[pl.ds(32, 32), :] = total[:, 64:]


def sum_line(got):
    return pl.pallas_call(
        sum_line_kernel,
        out_shape=jax.ShapeDtypeStruct((64, 64), F32),
        in_specs=[VMEM],
        out_specs=VMEM,
        name="sum_line",
    )(got)


def body(jacobian, smooth_x, smooth_y, smooth_z, index_x, index_y, index_z):
    sent = smooth_zy(jacobian, smooth_y, smooth_z, index_y, index_z)
    nz, ny, width = sent.shape
    got = lax.all_to_all(
        sent.reshape(128, nz * ny // 128, width), ("zh", "x", "zl", "y"), 0, 0, tiled=True
    )
    z = lax.axis_index(("zh", "x", "zl"))
    y0 = lax.axis_index("y") * 16
    core = lax.axis_index("core")
    panel = smooth_x_local(got, smooth_x, index_x, jnp.stack([z, y0]).astype(jnp.int32))
    own = panel.reshape(-1, panel.shape[2])
    other = lax.ppermute(own, "core", [(0, 1), (1, 0)])
    partial = gram(core.reshape(1).astype(jnp.int32), own, other)
    plane = lax.all_to_all(partial.reshape(16, 128, 256), ("x", "y"), 0, 0, tiled=True)
    line = lax.all_to_all(sum_plane(plane), ("zh", "zl"), 0, 0, tiled=True)
    return sum_line(line)


def solution(mesh):
    fine = Mesh(mesh.devices.reshape(2, 4, 2, 4, 4), ("zh", "x", "core", "zl", "y"))
    rows, cells = ("zh", "x", "core"), ("zl", "y")
    return jax.shard_map(
        body,
        mesh=fine,
        in_specs=(
            P(rows, cells, None, None),
            P(),
            P(),
            P(),
            P(),
            P(cells, None),
            P(cells, None),
        ),
        out_specs=P(rows, cells),
        check_vma=False,
    )
```

time: 405 us -> 109 us (0.27); the launches traced: 400 us -> 108 us
  waiting for transfers between devices: 257 us -> 32.1 us
  local copies, waits for them, and re-layouts: 54.1 us -> 5.3 us
  other arithmetic: 24.6 us -> 0.08 us
  Pallas kernels: 0 us -> 19.9 us
  between operations: 13.8 us -> 0.06 us
  matrix products: 9.38 us -> 0 us
  starting transfers between devices: 9.42 us -> 15.4 us
    all_gather x1 -> x0, waiting for transfers between devices: 175 us -> none  [body(): lax.all_gather(panel_rows, 'dp', axis=0, tiled=True)]
    unnamed x3 -> x0, waiting for transfers between devices: 74.4 us -> none
    gather x28 -> x0, local copies, waits for them, and re-layouts: 26.5 us -> none  [band_rows(): jnp.diagonal(padded, offset=shift_no, axis1=1, axis2=2)]
    all_to_all x1, waiting for transfers between devices: 7.53 us -> 29.5 us  [body(): lax.all_to_all(sent.reshape(128, nz * ny // 128, width), ('zh', 'x', 'zl'...]
    pallas_call x0 -> x5, Pallas kernels: none -> 19.9 us  [the longest x1 10.3 us: smooth_zy(): pl.pallas_call(zy_kernel, grid=(slab // planes,), out_shape=jax.ShapeDtyp...]
    add x4 -> x0, other arithmetic: 14.1 us -> none  [the longest x1 13.5 us: banded_apply(): running + coefs[shift_no][None] * lax.slice_in_dim(extended, shift_no, sh...]
    unnamed x1 -> x0, matrix products: 9.38 us -> none
    convert_element_type x2 -> x0, other arithmetic: 8.88 us -> none  [short(): return part.astype(jnp.bfloat16) if part.dtype == jnp.float32 else part]
  transfers between devices with their start and end apart: 3 -> 2, of which waited for: 3 -> 2; matrix products, arithmetic and copies ran while one was open for 4% -> 0% of each run, Pallas kernels for 0% -> 0%
where the time goes in v1:
time: 109 us; the launch traced here: 108 us
  blocking collectives  35.6 us (33%)
  waiting for transfers between devices  32.1 us (29%)
  Pallas kernels  19.9 us (18%)
  starting transfers between devices  15.4 us (14%)
  local copies, waits for them, and re-layouts  5.3 us (5%)
    all_to_all x1, waiting for transfers between devices, body(): lax.all_to_all(sent.reshape(128, nz * ny // 128, width), ('zh', 'x', 'zl'...  29.5 us
    all_to_all x1, blocking collectives, body(): lax.all_to_all(partial.reshape(16, 128, 256), ('x', 'y'), 0, 0, tiled=True)  22.6 us
    all_to_all x1, starting transfers between devices, body(): lax.all_to_all(sent.reshape(128, nz * ny // 128, width), ('zh', 'x', 'zl'...  15.3 us
    all_to_all x1, blocking collectives, body(): line = lax.all_to_all(sum_plane(plane), ('zh', 'zl'), 0, 0, tiled=True)  13.1 us
    pallas_call x1, Pallas kernels, smooth_zy(): pl.pallas_call(zy_kernel, grid=(slab // planes,), out_shape=jax.ShapeDtyp...  10.3 us
    unnamed x14, local copies, waits for them, and re-layouts  5.3 us
    pallas_call x1, Pallas kernels, smooth_x_local(): pl.pallas_call(x_kernel, out_shape=jax.ShapeDtypeStruct((nx, columns, 512...  4.55 us
    ppermute x1, waiting for transfers between devices, body(): other = lax.ppermute(own, 'core', [(0, 1), (1, 0)])  2.64 us
  transfers between devices with their start and end apart: 2, of which 2 were waited for; matrix products, arithmetic and copies ran while one was open for 0% of the time, Pallas kernels for 0%

profile of v1, /device:TPU:8, one launch (start us, length us, event | category | flops | bytes accessed | tf_op | source)
XLA Modules:
  0.0 108.5 jit_solution(8539776122042388736)
XLA Ops:
  0.0 0.0 copy-start
  0.0 2.2 %copy-done = f32[64,4,64,32]{2,3,1,0:T(8,128)S(1)} copy-done((f32[64,4,64,32]{2,3,1,0:T(8,128)S(1)}, f32[64,4,64,32]{2,3,1,0:T(8,128)}, u32[]{:S(2)}) %copy-start) | copy-done | bytes 2097176
  2.2 0.0 copy-start.1
  2.2 0.9 copy-done.1
  3.1 0.0 copy-start.3
  3.1 0.8 copy-done.3
  3.9 0.0 copy-start.5
  3.9 0.7 copy-done.5
  4.6 0.7 copy-done.6
  5.3 0.0 copy-start.2
  5.3 10.3 %smooth_zy.1 = bf16[32,64,256]{2,1,0:T(8,128)(2,1)} custom-call(s32[4,32]{1,0:T(4,128)S(1)} %copy-done.5, s32[4,64]{1,0:T(4,128)S(1)} %copy-done.6, f32[4,64,64]{2,1,0:T(8,128)S(1)} %copy-done.1, f32[4,32,32]{2,1,0:T(8,128)S(1)} %copy-done.3, f32[64,4,32,64]{3,2,1,0:T(8,128)S(1)} %bitcast.10), custom_call_target="tpu_custom_call" | custom-call | tf_op jit(solution)/shard_map/smooth_zy/pallas_call | solution.py:76
  15.6 15.3 %all-to-all-start = ((bf16[128,16,256]{2,1,0:T(8,128)(2,1)}), bf16[128,16,256]{2,1,0:T(8,128)(2,1)S(1)}, u32[]{:S(2)}, u32[]{:S(2)}) async-start(bf16[128,16,256]{2,1,0:T(8,128)(2,1)} %bitcast.5), calls=%async_computation | async-start | bytes 2097152 | tf_op jit(solution)/shard_map/all_to_all | solution.py:229
  31.0 0.1 pad_add_fusion.place
  31.1 29.5 %all-to-all-done.got = bf16[128,16,256]{2,1,0:T(8,128)(2,1)S(1)} async-done(((bf16[128,16,256]{2,1,0:T(8,128)(2,1)}), bf16[128,16,256]{2,1,0:T(8,128)(2,1)S(1)}, u32[]{:S(2)}, u32[]{:S(2)}) %all-to-all-start) | async-done | bytes 1048608 | tf_op jit(solution)/shard_map/all_to_all | solution.py:229
  60.5 0.0 copy-done.2
  60.5 0.0 copy-done.4
  60.5 4.6 %smooth_x.1 = bf16[64,16,512]{2,1,0:T(8,128)(2,1)S(1)} custom-call(s32[2]{0:T(128)S(1)} %pad_add_fusion.place, s32[32,64]{1,0:T(8,128)S(1)} %bitcast.12, f32[4,64,64]{2,1,0:T(8,128)S(1)} %copy-done.2, bf16[128,16,256]{2,1,0:T(8,128)(2,1)S(1)} %all-to-all-done.got), custom_call_target="tpu_custom_call" | custom-call | tf_op jit(solution)/shard_map/smooth_x/pallas_call | solution.py:145
  65.1 0.1 collective-permute-start
  65.2 2.6 %collective-permute-done.other = bf16[1024,512]{1,0:T(8,128)(2,1)S(1)} collective-permute-done((bf16[1024,512]{1,0:T(8,128)(2,1)S(1)}, bf16[1024,512]{1,0:T(8,128)(2,1)S(1)}, u32[]{:S(2)}, u32[]{:S(2)}) %collective-permute-start) | collective-permute-done | bytes 1048608 | tf_op jit(solution)/shard_map/ppermute | solution.py:237
  67.8 1.3 %gram.1 = bf16[4,4,128,256]{3,2,1,0:T(8,128)(2,1)S(1)} custom-call(s32[1]{0:T(128)} %bitcast.core, bf16[1024,512]{1,0:T(8,128)(2,1)S(1)} %bitcast.9, bf16[1024,512]{1,0:T(8,128)(2,1)S(1)} %collective-permute-done.other), custom_call_target="tpu_custom_call" | custom-call | tf_op jit(solution)/shard_map/gram/pallas_call | solution.py:178
  69.1 22.6 %all_to_all.15.got = bf16[16,128,256]{2,1,0:T(8,128)(2,1)} all-to-all(bf16[16,128,256]{2,1,0:T(8,128)(2,1)S(1)} %bitcast.11), channel_id=1, replica_groups=mesh['zh'=2,'x'=4,'core'=2,'zl'=4,'y'=4] {'x','y'}, dimensions={0} | all-to-all | bytes 2097152 | tf_op jit(solution)/shard_map/all_to_all | solution.py:239
  91.7 2.1 %sum_plane.1 = f32[8,32,128]{2,1,0:T(8,128)} custom-call(bf16[16,128,256]{2,1,0:T(8,128)(2,1)} %all_to_all.15.got), custom_call_target="tpu_custom_call" | custom-call | tf_op jit(solution)/shard_map/sum_plane/pallas_call | solution.py:199
  93.8 13.1 %all_to_all.16.got = f32[8,32,128]{2,1,0:T(8,128)} all-to-all(f32[8,32,128]{2,1,0:T(8,128)} %sum_plane.1), channel_id=1, replica_groups=mesh['zh'=2,'x'=4,'core'=2,'zl'=4,'y'=4] {'zh','zl'}, dimensions={0} | all-to-all | bytes 262144 | tf_op jit(solution)/shard_map/all_to_all | solution.py:240
  106.9 1.6 %sum_line.1 = f32[64,64]{1,0:T(8,128)} custom-call(f32[8,32,128]{2,1,0:T(8,128)} %all_to_all.16.got), custom_call_target="tpu_custom_call" | custom-call | tf_op jit(solution)/shard_map/sum_line/pallas_call | solution.py:217
  (2 shorter events, 0.0 us)
Async XLA Ops:
  0.0 2.2 %copy-start = (f32[64,4,64,32]{2,3,1,0:T(8,128)S(1)}, f32[64,4,64,32]{2,3,1,0:T(8,128)}, u32[]{:S(2)}) copy-start(f32[64,4,64,32]{2,3,1,0:T(8,128)} %param.7) | copy-start | bytes 6291460
  2.2 0.9 copy-start.1
  3.1 0.8 copy-start.3
  3.9 0.7 copy-start.5
  4.6 0.7 copy-start.6
  5.3 55.2 %copy-start.2 = (f32[4,64,64]{2,1,0:T(8,128)S(1)}, f32[4,64,64]{2,1,0:T(8,128)}, u32[]{:S(2)}) copy-start(f32[4,64,64]{2,1,0:T(8,128)} %table_x.1) | copy-start | bytes 196612
  5.3 55.2 %copy-start.4 = (s32[64,32]{0,1:T(8,128)S(1)}, s32[64,32]{0,1:T(8,128)}, u32[]{:S(2)}) copy-start(s32[64,32]{0,1:T(8,128)} %param.11) | copy-start | bytes 24580
  15.6 44.9 %all-to-all-start = ((bf16[128,16,256]{2,1,0:T(8,128)(2,1)}), bf16[128,16,256]{2,1,0:T(8,128)(2,1)S(1)}, u32[]{:S(2)}, u32[]{:S(2)}) async-start(bf16[128,16,256]{2,1,0:T(8,128)(2,1)} %bitcast.5), calls=%async_computation | async-start | bytes 2097152 | tf_op jit(solution)/shard_map/all_to_all | solution.py:229
  65.1 2.7 %collective-permute-start = (bf16[1024,512]{1,0:T(8,128)(2,1)S(1)}, bf16[1024,512]{1,0:T(8,128)(2,1)S(1)}, u32[]{:S(2)}, u32[]{:S(2)}) collective-permute-start(bf16[1024,512]{1,0:T(8,128)(2,1)S(1)} %bitcast.8), channel_id=1, source_target_pairs={{0,16},{16,0},{1,17},{17,1},{2,18},{18,2},{3,19},{19,3},{4,20},{20... | collective-permute-start | bytes 3145736 | tf_op jit(solution)/shard_map/ppermute | solution.py:237

commit v2 on v1

--- a/solution.py
+++ b/solution.py
@@ -115,8 +115,8 @@
     def _(cell):
         for parity in range(2):
             for zh in range(2):
-                first = (zh * 4 + parity) * cells + cell
-                second = (zh * 4 + 2 + parity) * cells + cell
+                first = zh * 64 + cell // 4 * 16 + parity * 4 + cell % 4
+                second = first + 8
                 lanes = pl.ds((parity * 2 + zh) * 128, 128)
                 for pair in range(per // 2):
                     a = got[first, :, pl.ds(pair * 128, 128)].astype(F32)
@@ -159,25 +159,33 @@
 def gram_kernel(core, own, other, out):
     mine = core[0]
     left = own[...]
+    low = lax.broadcasted_iota(jnp.int32, (32, 128), 1) < 64
     for k, right in enumerate((own, other)):
         which = mine if k == 0 else 1 - mine
         for part in range(2):
-            piece = lax.dot_general(
+            whole = lax.dot_general(
                 left,
                 right[:, part * 256 : (part + 1) * 256],
                 (((0,), (0,)), ((), ())),
                 preferred_element_type=F32,
-            ).astype(BF16)
+            )
             for x in range(4):
                 for zh in range(2):
                     start = ((x % 2 * 2 + zh) * 2 + x // 2) * 64
-                    out[x, part * 2 + which, pl.ds(zh * 64, 64), :] = piece[start : start + 64]
+                    for pair in range(2):
+                        lanes = slice(pair * 128, pair * 128 + 128)
+                        upper = whole[start : start + 32, lanes]
+                        lower = whole[start + 32 : start + 64, lanes]
+                        first = jnp.where(low, upper, pltpu.roll(lower, 64, 1))
+                        second = jnp.where(low, pltpu.roll(upper, 64, 1), lower)
+                        out[zh, pair * 2, x, part * 2 + which] = first.astype(BF16)
+                        out[zh, pair * 2 + 1, x, part * 2 + which] = second.astype(BF16)
 
 
 def gram(core, own, other):
     return pl.pallas_call(
         gram_kernel,
-        out_shape=jax.ShapeDtypeStruct((4, 4, 128, 256), BF16),
+        out_shape=jax.ShapeDtypeStruct((2, 4, 4, 4, 32, 128), BF16),
         in_specs=[SMEM, VMEM, VMEM],
         out_specs=VMEM,
         compiler_params=pltpu.CompilerParams(vmem_limit_bytes=40 * 2**20),
@@ -185,60 +193,38 @@
     )(core, own, other)
 
 
-def sum_plane_kernel(got, out):
+def sum_kernel(got, out):
     total = got[0].astype(F32)
     for k in range(1, got.shape[0]):
         total = total + got[k].astype(F32)
-    for zh in range(2):
-        for zl in range(4):
-            block = total[zh * 64 : (zh + 1) * 64, zl * 64 : (zl + 1) * 64]
-            out[zh * 4 + zl] = jnp.concatenate([block[:32], block[32:]], axis=1)
-
-
-def sum_plane(got):
-    return pl.pallas_call(
-        sum_plane_kernel,
-        out_shape=jax.ShapeDtypeStruct((8, 32, 128), F32),
-        in_specs=[VMEM],
-        out_specs=VMEM,
-        name="sum_plane",
-    )(got)
-
-
-def sum_line_kernel(got, out):
-    total = got[0]
-    for k in range(1, got.shape[0]):
-        total = total + got[k]
     out[pl.ds(0, 32), :] = total[:, :64]
     out[pl.ds(32, 32), :] = total[:, 64:]
 
 
-def sum_line(got):
-    return pl.pallas_call(
-        sum_line_kernel,
+def sum_parts(got):
+    return pl.pallas_call(
+        sum_kernel,
         out_shape=jax.ShapeDtypeStruct((64, 64), F32),
         in_specs=[VMEM],
         out_specs=VMEM,
-        name="sum_line",
+        name="sum_parts",
     )(got)
 
 
 def body(jacobian, smooth_x, smooth_y, smooth_z, index_x, index_y, index_z):
+    chips = ("zh", "zl", "x", "y")
     sent = smooth_zy(jacobian, smooth_y, smooth_z, index_y, index_z)
     nz, ny, width = sent.shape
-    got = lax.all_to_all(
-        sent.reshape(128, nz * ny // 128, width), ("zh", "x", "zl", "y"), 0, 0, tiled=True
-    )
-    z = lax.axis_index(("zh", "x", "zl"))
+    got = lax.all_to_all(sent.reshape(128, nz * ny // 128, width), chips, 0, 0, tiled=True)
+    z = lax.axis_index(("zh", "zl", "x"))
     y0 = lax.axis_index("y") * 16
     core = lax.axis_index("core")
     panel = smooth_x_local(got, smooth_x, index_x, jnp.stack([z, y0]).astype(jnp.int32))
     own = panel.reshape(-1, panel.shape[2])
     other = lax.ppermute(own, "core", [(0, 1), (1, 0)])
     partial = gram(core.reshape(1).astype(jnp.int32), own, other)
-    plane = lax.all_to_all(partial.reshape(16, 128, 256), ("x", "y"), 0, 0, tiled=True)
-    line = lax.all_to_all(sum_plane(plane), ("zh", "zl"), 0, 0, tiled=True)
-    return sum_line(line)
+    parts = lax.all_to_all(partial.reshape(128, 32, 128), chips, 0, 0, tiled=True)
+    return sum_parts(parts)
 
 
 def solution(mesh):

time: 109 us -> 111 us (1.018)
  blocking collectives: 35.6 us -> 38.1 us
  Pallas kernels: 19.9 us -> 18.4 us
    all_to_all x2 -> x1, blocking collectives: 35.6 us -> 38.1 us  [body(): lax.all_to_all(partial.reshape(128, 32, 128), chips, 0, 0, tiled=True)]
    pallas_call x3 -> x2, Pallas kernels: 4.99 us -> 3.48 us  [the longest x1 2.11 us: sum_parts(): pl.pallas_call(sum_kernel, out_shape=jax.ShapeDtypeStruct((64, 64), F32),...]
where the time goes in v2:
time: 111 us; the launch traced here: 110 us
  blocking collectives  38.1 us (34%)
  waiting for transfers between devices  33.2 us (30%)
  Pallas kernels  18.4 us (17%)
  starting transfers between devices  15.4 us (14%)
  local copies, waits for them, and re-layouts  5.3 us (5%)
    all_to_all x1, blocking collectives, body(): lax.all_to_all(partial.reshape(128, 32, 128), chips, 0, 0, tiled=True)  38.1 us
    all_to_all x1, waiting for transfers between devices, body(): lax.all_to_all(sent.reshape(128, nz * ny // 128, width), chips, 0, 0, til...  30.5 us
    all_to_all x1, starting transfers between devices, body(): lax.all_to_all(sent.reshape(128, nz * ny // 128, width), chips, 0, 0, til...  15.3 us
    pallas_call x1, Pallas kernels, smooth_zy(): pl.pallas_call(zy_kernel, grid=(slab // planes,), out_shape=jax.ShapeDtyp...  10.3 us
    unnamed x14, local copies, waits for them, and re-layouts  5.3 us
    pallas_call x1, Pallas kernels, smooth_x_local(): pl.pallas_call(x_kernel, out_shape=jax.ShapeDtypeStruct((nx, columns, 512...  4.59 us
    ppermute x1, waiting for transfers between devices, body(): other = lax.ppermute(own, 'core', [(0, 1), (1, 0)])  2.64 us
  transfers between devices with their start and end apart: 2, of which 2 were waited for; matrix products, arithmetic and copies ran while one was open for 0% of the time, Pallas kernels for 0%

profile of v2, /device:TPU:8, one launch (start us, length us, event | category | flops | bytes accessed | tf_op | source)
XLA Modules:
  0.0 110.5 jit_solution(182345756615977036)
XLA Ops:
  0.0 0.0 copy-start
  0.0 2.2 %copy-done = f32[64,4,64,32]{2,3,1,0:T(8,128)S(1)} copy-done((f32[64,4,64,32]{2,3,1,0:T(8,128)S(1)}, f32[64,4,64,32]{2,3,1,0:T(8,128)}, u32[]{:S(2)}) %copy-start) | copy-done | bytes 2097176
  2.2 0.0 copy-start.1
  2.2 0.9 copy-done.1
  3.1 0.0 copy-start.3
  3.1 0.8 copy-done.3
  3.9 0.0 copy-start.5
  3.9 0.7 copy-done.5
  4.6 0.0 copy-start.6
  4.6 0.7 copy-done.6
  5.3 0.0 copy-start.2
  5.3 0.0 copy-start.4
  5.3 10.3 %smooth_zy.1 = bf16[32,64,256]{2,1,0:T(8,128)(2,1)} custom-call(s32[4,32]{1,0:T(4,128)S(1)} %copy-done.5, s32[4,64]{1,0:T(4,128)S(1)} %copy-done.6, f32[4,64,64]{2,1,0:T(8,128)S(1)} %copy-done.1, f32[4,32,32]{2,1,0:T(8,128)S(1)} %copy-done.3, f32[64,4,32,64]{3,2,1,0:T(8,128)S(1)} %bitcast.10), custom_call_target="tpu_custom_call" | custom-call | tf_op jit(solution)/shard_map/smooth_zy/pallas_call | solution.py:76
  15.6 15.3 %all-to-all-start = ((bf16[128,16,256]{2,1,0:T(8,128)(2,1)}), bf16[128,16,256]{2,1,0:T(8,128)(2,1)S(1)}, u32[]{:S(2)}, u32[]{:S(2)}) async-start(bf16[128,16,256]{2,1,0:T(8,128)(2,1)} %bitcast.5), calls=%async_computation | async-start | bytes 2097152 | tf_op jit(solution)/shard_map/all_to_all | solution.py:218
  31.0 0.1 pad_add_fusion.place
  31.1 30.5 %all-to-all-done.got = bf16[128,16,256]{2,1,0:T(8,128)(2,1)S(1)} async-done(((bf16[128,16,256]{2,1,0:T(8,128)(2,1)}), bf16[128,16,256]{2,1,0:T(8,128)(2,1)S(1)}, u32[]{:S(2)}, u32[]{:S(2)}) %all-to-all-start) | async-done | bytes 1048608 | tf_op jit(solution)/shard_map/all_to_all | solution.py:218
  61.6 0.0 copy-done.2
  61.6 0.0 copy-done.4
  61.6 4.6 %smooth_x.1 = bf16[64,16,512]{2,1,0:T(8,128)(2,1)S(1)} custom-call(s32[2]{0:T(128)S(1)} %pad_add_fusion.place, s32[32,64]{1,0:T(8,128)S(1)} %bitcast.12, f32[4,64,64]{2,1,0:T(8,128)S(1)} %copy-done.2, bf16[128,16,256]{2,1,0:T(8,128)(2,1)S(1)} %all-to-all-done.got), custom_call_target="tpu_custom_call" | custom-call | tf_op jit(solution)/shard_map/smooth_x/pallas_call | solution.py:145
  66.2 0.1 collective-permute-start
  66.3 2.6 %collective-permute-done.other = bf16[1024,512]{1,0:T(8,128)(2,1)S(1)} collective-permute-done((bf16[1024,512]{1,0:T(8,128)(2,1)S(1)}, bf16[1024,512]{1,0:T(8,128)(2,1)S(1)}, u32[]{:S(2)}, u32[]{:S(2)}) %collective-permute-start) | collective-permute-done | bytes 1048608 | tf_op jit(solution)/shard_map/ppermute | solution.py:224
  69.0 1.4 %gram.1 = bf16[2,4,4,4,32,128]{5,4,3,2,1,0:T(8,128)(2,1)S(1)} custom-call(s32[1]{0:T(128)} %bitcast.core, bf16[1024,512]{1,0:T(8,128)(2,1)S(1)} %bitcast.9, bf16[1024,512]{1,0:T(8,128)(2,1)S(1)} %collective-permute-done.other), custom_call_target="tpu_custom_call" | custom-call | tf_op jit(solution)/shard_map/gram/pallas_call | solution.py:186
  70.3 38.1 %all_to_all.10.got = bf16[128,32,128]{2,1,0:T(8,128)(2,1)} all-to-all(bf16[128,32,128]{2,1,0:T(8,128)(2,1)S(1)} %bitcast.11), channel_id=1, replica_groups=mesh['zh'=2,'x'=4,'core'=2,'zl'=4,'y'=4] {'zh','zl','x','y'}, dimensions={0} | all-to-all | bytes 2097152 | tf_op jit(solution)/shard_map/all_to_all | solution.py:226
  108.4 2.1 %sum_parts.1 = f32[64,64]{1,0:T(8,128)} custom-call(bf16[128,32,128]{2,1,0:T(8,128)(2,1)} %all_to_all.10.got), custom_call_target="tpu_custom_call" | custom-call | tf_op jit(solution)/shard_map/sum_parts/pallas_call | solution.py:205
Async XLA Ops:
  0.0 2.2 %copy-start = (f32[64,4,64,32]{2,3,1,0:T(8,128)S(1)}, f32[64,4,64,32]{2,3,1,0:T(8,128)}, u32[]{:S(2)}) copy-start(f32[64,4,64,32]{2,3,1,0:T(8,128)} %param.7) | copy-start | bytes 6291460
  2.2 0.9 copy-start.1
  3.1 0.8 copy-start.3
  3.9 0.7 copy-start.5
  4.6 0.7 copy-start.6
  5.3 56.3 %copy-start.2 = (f32[4,64,64]{2,1,0:T(8,128)S(1)}, f32[4,64,64]{2,1,0:T(8,128)}, u32[]{:S(2)}) copy-start(f32[4,64,64]{2,1,0:T(8,128)} %table_x.1) | copy-start | bytes 196612
  5.3 56.3 %copy-start.4 = (s32[64,32]{0,1:T(8,128)S(1)}, s32[64,32]{0,1:T(8,128)}, u32[]{:S(2)}) copy-start(s32[64,32]{0,1:T(8,128)} %param.11) | copy-start | bytes 24580
  15.6 46.0 %all-to-all-start = ((bf16[128,16,256]{2,1,0:T(8,128)(2,1)}), bf16[128,16,256]{2,1,0:T(8,128)(2,1)S(1)}, u32[]{:S(2)}, u32[]{:S(2)}) async-start(bf16[128,16,256]{2,1,0:T(8,128)(2,1)} %bitcast.5), calls=%async_computation | async-start | bytes 2097152 | tf_op jit(solution)/shard_map/all_to_all | solution.py:218
  66.2 2.7 %collective-permute-start = (bf16[1024,512]{1,0:T(8,128)(2,1)S(1)}, bf16[1024,512]{1,0:T(8,128)(2,1)S(1)}, u32[]{:S(2)}, u32[]{:S(2)}) collective-permute-start(bf16[1024,512]{1,0:T(8,128)(2,1)S(1)} %bitcast.8), channel_id=1, source_target_pairs={{0,16},{16,0},{1,17},{17,1},{2,18},{18,2},{3,19},{19,3},{4,20},{20... | collective-permute-start | bytes 3145736 | tf_op jit(solution)/shard_map/ppermute | solution.py:224

commit v3 on v1

v3 whole, which is shorter than its diff:
```python
import jax
import jax.numpy as jnp
from jax import lax
from jax.experimental import pallas as pl
from jax.experimental.pallas import tpu as pltpu
from jax.sharding import Mesh, PartitionSpec as P

BAND = 3
TAPS = 2 * BAND + 1
TABLES = 4
GROUP = 8
AHEAD = 3
F32 = jnp.float32
BF16 = jnp.bfloat16
VMEM = pl.BlockSpec(memory_space=pltpu.VMEM)
SMEM = pl.BlockSpec(memory_space=pltpu.SMEM)
HBM = pl.BlockSpec(memory_space=pltpu.HBM)


def split_table(table):
    high = table.astype(BF16)
    low = (table - high.astype(F32)).astype(BF16)
    return high, low


def band_column(table, tap):
    rows = lax.broadcasted_iota(jnp.int32, table.shape, 0)
    cols = lax.broadcasted_iota(jnp.int32, table.shape, 1)
    return jnp.sum(jnp.where(cols == rows + (tap - BAND), table, 0.0), axis=1, keepdims=True)


def zy_kernel(jac, table_y, table_z, index_y, index_z, out, planes, coef, lhs, ty, tz, iy, iz, sems, small):
    slab, nz, rows, ny = planes.shape
    loads = [
        pltpu.make_async_copy(s, d, small.at[k])
        for k, (s, d) in enumerate(((table_z, tz), (index_z, iz), (table_y, ty), (index_y, iy)))
    ]
    for load in loads:
        load.start()
    waves = []
    for x0 in range(0, slab, 2):
        for w0 in range(0, nz, GROUP):
            waves.append([(x, w) for w in range(w0, w0 + GROUP) for x in (x0, x0 + 1)])
    copies = {}
    started, waited = [0], [0]

    def start_until(count):
        while started[0] < min(count, len(waves)):
            for x, w in waves[started[0]]:
                copies[x, w] = pltpu.make_async_copy(jac.at[:, x, w, :], planes.at[x, w], sems.at[x, w])
                copies[x, w].start()
            started[0] += 1

    def wait_until(count):
        while waited[0] < min(count, len(waves)):
            for x, w in waves[waited[0]]:
                copies[x, w].wait()
            waited[0] += 1

    start_until(AHEAD)
    loads[0].wait()
    loads[1].wait()
    for tap in range(TAPS):
        cols = [band_column(tz[t], tap) for t in range(TABLES)]
        for x in range(slab):
            label = iz[pl.ds(x, 1), :]
            picked = jnp.broadcast_to(cols[0], (nz, ny))
            for t in range(1, TABLES):
                picked = jnp.where(label == t, cols[t], picked)
            coef[x, tap] = picked
    loads[2].wait()
    loads[3].wait()
    for t in range(TABLES):
        high, low = split_table(ty[t])
        lhs[pl.ds(t * ny, ny), :] = jnp.concatenate([high, low], axis=1)
    left = lhs[...]
    lane = lax.broadcasted_iota(jnp.int32, (1, 2 * rows), 1)
    half = rows // 2

    def finish(both, z, x0):
        for k, zz in enumerate((z, z + 1)):
            label = jnp.where(lane < rows, iy[x0, zz], iy[x0 + 1, zz])
            part = both[:, k * 2 * rows : (k + 1) * 2 * rows]
            picked = part[:ny]
            for t in range(1, TABLES):
                picked = jnp.where(label == t, part[t * ny : (t + 1) * ny], picked)
            out[zz, :, pl.ds(x0 * rows, 2 * rows)] = picked.astype(BF16)

    pending = []
    for x0 in range(0, slab, 2):
        for z in range(0, nz, 2):
            per = nz // GROUP
            need = x0 // 2 * per + min(z + BAND + 1, nz - 1) // GROUP + 1
            start_until(need + AHEAD - 1)
            wait_until(need)
            parts = {}
            for x in (x0, x0 + 1):
                for h in range(2):
                    use = pl.ds(h * half, half)
                    held = {w: planes[x, w, use, :] for w in range(max(z - BAND, 0), min(z + BAND + 2, nz))}
                    for zz in (z, z + 1):
                        total = None
                        for w in range(max(zz - BAND, 0), min(zz + BAND + 1, nz)):
                            term = coef[x, w - zz + BAND, pl.ds(zz, 1), :] * held[w]
                            total = term if total is None else total + term
                        short = total.astype(BF16)
                        parts[zz, x, h] = jnp.concatenate([short, short], axis=1)
            rhs = jnp.concatenate([parts[zz, x, h] for zz in (z, z + 1) for x in (x0, x0 + 1) for h in range(2)], axis=0)
            both = lax.dot_general(left, rhs, (((1,), (1,)), ((), ())), preferred_element_type=F32)
            pending.append((both, z, x0))
            if len(pending) > 1:
                finish(*pending.pop(0))
    for item in pending:
        finish(*item)


def smooth_zy(jacobian, smooth_y, smooth_z, index_y, index_z):
    rows, slab, ny, nz = jacobian.shape
    return pl.pallas_call(
        zy_kernel,
        out_shape=jax.ShapeDtypeStruct((nz, ny, slab * rows), BF16),
        in_specs=[HBM] * 5,
        out_specs=VMEM,
        scratch_shapes=[
            pltpu.VMEM((slab, nz, rows, ny), F32),
            pltpu.VMEM((slab, TAPS, nz, ny), F32),
            pltpu.VMEM((TABLES * ny, 2 * ny), BF16),
            pltpu.VMEM(smooth_y.shape, F32),
            pltpu.VMEM(smooth_z.shape, F32),
            pltpu.SMEM(index_y.shape, jnp.int32),
            pltpu.VMEM(index_z.shape, jnp.int32),
            pltpu.SemaphoreType.DMA((slab, nz)),
            pltpu.SemaphoreType.DMA((4,)),
        ],
        compiler_params=pltpu.CompilerParams(vmem_limit_bytes=60 * 2**20),
        name="smooth_zy",
    )(jnp.swapaxes(jacobian, 2, 3), smooth_y, smooth_z, index_y, index_z)


def coef_kernel(place, index_x, table_x, out, bands):
    z, y0 = place[0], place[1]
    nx, taps, columns, lanes = out.shape
    for t in range(TABLES):
        for tap in range(taps):
            bands[t, tap] = jnp.broadcast_to(band_column(table_x[t], tap), (nx, lanes))
    row = index_x[pl.ds(z, 1), :]
    sub = lax.broadcasted_iota(jnp.int32, (columns, row.shape[1]), 0)
    lan = lax.broadcasted_iota(jnp.int32, (columns, row.shape[1]), 1)
    label = jnp.sum(jnp.where(lan == sub + y0, row, 0).astype(F32), axis=1, keepdims=True)
    label = jnp.broadcast_to(label, (columns, lanes))

    @pl.loop(0, nx)
    def _(x):
        for tap in range(taps):
            picked = jnp.broadcast_to(bands[0, tap, pl.ds(x, 1), :], label.shape)
            for t in range(1, TABLES):
                picked = jnp.where(label == t, bands[t, tap, pl.ds(x, 1), :], picked)
            out[x, tap] = picked


def x_coefs(place, index_x, smooth_x):
    nx = smooth_x.shape[1]
    return pl.pallas_call(
        coef_kernel,
        out_shape=jax.ShapeDtypeStruct((nx, TAPS, 16, 128), F32),
        in_specs=[SMEM, VMEM, VMEM],
        out_specs=VMEM,
        scratch_shapes=[pltpu.VMEM((TABLES, TAPS, nx, 128), F32)],
        compiler_params=pltpu.CompilerParams(vmem_limit_bytes=12 * 2**20),
        cost_estimate=pl.CostEstimate(flops=4 * 2**20, bytes_accessed=4 * 2**20, transcendentals=0),
        name="x_coefs",
    )(place, jnp.swapaxes(index_x, 0, 1), smooth_x)


def x_kernel(coef, got, out, wide):
    nx, columns, lanes = out.shape
    left = lax.broadcasted_iota(jnp.int32, (columns, 128), 1) < 64
    for edge in range(BAND):
        wide[edge] = jnp.zeros(wide.shape[1:], F32)
        wide[nx + BAND + edge] = jnp.zeros(wide.shape[1:], F32)

    def merge(cell, carry):
        for parity in range(2):
            for zh in range(2):
                first = zh * 64 + cell // 4 * 16 + parity * 4 + cell % 4
                second = first + 8
                use = pl.ds((parity * 2 + zh) * 128, 128)
                for pair in range(2):
                    a = got[first, :, pl.ds(pair * 128, 128)].astype(F32)
                    b = got[second, :, pl.ds(pair * 128, 128)].astype(F32)
                    base = cell * 4 + pair * 2 + BAND
                    wide[base, :, use] = jnp.where(left, a, pltpu.roll(b, 64, 1))
                    wide[base + 1, :, use] = jnp.where(left, pltpu.roll(a, 64, 1), b)
        return carry

    def smooth(step, carry):
        x = step * 2
        for block in range(lanes // 128):
            use = pl.ds(block * 128, 128)
            held = [wide[x + k, :, use] for k in range(TAPS + 1)]
            for k in range(2):
                total = coef[x + k, 0] * held[k]
                for tap in range(1, TAPS):
                    total = total + coef[x + k, tap] * held[k + tap]
                out[x + k, :, use] = total.astype(BF16)
        return carry

    lax.fori_loop(0, nx // 4, merge, 0, unroll=16)
    lax.fori_loop(0, nx // 2, smooth, 0, unroll=8)


def smooth_x_local(coef, got):
    nx, _, columns, _ = coef.shape
    return pl.pallas_call(
        x_kernel,
        out_shape=jax.ShapeDtypeStruct((nx, columns, 512), BF16),
        in_specs=[VMEM, VMEM],
        out_specs=VMEM,
        scratch_shapes=[pltpu.VMEM((nx + 2 * BAND, columns, 512), F32)],
        compiler_params=pltpu.CompilerParams(vmem_limit_bytes=12 * 2**20),
        name="smooth_x",
    )(coef, got)


def add_up(parts):
    while len(parts) > 1:
        parts = [a + b for a, b in zip(parts[::2], parts[1::2])] + parts[len(parts) // 2 * 2 :]
    return parts[0]


def gram_kernel(core, own, other, out):
    mine = core[0]
    left = own[...]
    for k, right in enumerate((own, other)):
        which = mine if k == 0 else 1 - mine
        for part in range(2):
            piece = lax.dot_general(
                left,
                right[:, part * 256 : (part + 1) * 256],
                (((0,), (0,)), ((), ())),
                preferred_element_type=F32,
            ).astype(BF16)
            for x in range(4):
                for zh in range(2):
                    start = ((x % 2 * 2 + zh) * 2 + x // 2) * 64
                    out[x, part * 2 + which, pl.ds(zh * 64, 64), :] = piece[start : start + 64]


def gram(core, own, other):
    return pl.pallas_call(
        gram_kernel,
        out_shape=jax.ShapeDtypeStruct((4, 4, 128, 256), BF16),
        in_specs=[SMEM, VMEM, VMEM],
        out_specs=VMEM,
        compiler_params=pltpu.CompilerParams(vmem_limit_bytes=16 * 2**20),
        name="gram",
    )(core, own, other)


def sum_plane_kernel(got, out):
    for zh in range(2):
        for pair in range(2):
            rows, lanes = pl.ds(zh * 64, 64), pl.ds(pair * 128, 128)
            total = add_up([got[k, rows, lanes].astype(F32) for k in range(got.shape[0])])
            left = lax.broadcasted_iota(jnp.int32, (32, 128), 1) < 64
            upper, lower = total[:32], total[32:]
            out[zh * 4 + pair * 2] = jnp.where(left, upper, pltpu.roll(lower, 64, 1))
            out[zh * 4 + pair * 2 + 1] = jnp.where(left, pltpu.roll(upper, 64, 1), lower)


def sum_plane(got):
    return pl.pallas_call(
        sum_plane_kernel,
        out_shape=jax.ShapeDtypeStruct((8, 32, 128), F32),
        in_specs=[VMEM],
        out_specs=VMEM,
        compiler_params=pltpu.CompilerParams(vmem_limit_bytes=8 * 2**20),
        name="sum_plane",
    )(got)


def sum_line_kernel(got, out):
    total = add_up([got[k] for k in range(got.shape[0])])
    out[pl.ds(0, 32), :] = total[:, :64]
    out[pl.ds(32, 32), :] = total[:, 64:]


def sum_line(got):
    return pl.pallas_call(
        sum_line_kernel,
        out_shape=jax.ShapeDtypeStruct((64, 64), F32),
        in_specs=[VMEM],
        out_specs=VMEM,
        compiler_params=pltpu.CompilerParams(vmem_limit_bytes=4 * 2**20),
        name="sum_line",
    )(got)


def body(jacobian, smooth_x, smooth_y, smooth_z, index_x, index_y, index_z):
    sent = smooth_zy(jacobian, smooth_y, smooth_z, index_y, index_z)
    nz, ny, width = sent.shape
    place = jnp.stack([lax.axis_index(("zh", "zl", "x")), lax.axis_index("y") * 16]).astype(jnp.int32)
    coef = x_coefs(place, index_x, smooth_x)
    got = lax.all_to_all(
        sent.reshape(128, nz * ny // 128, width), ("zh", "zl", "x", "y"), 0, 0, tiled=True
    )
    panel = smooth_x_local(coef, got)
    own = panel.reshape(-1, panel.shape[2])
    other = lax.ppermute(own, "core", [(0, 1), (1, 0)])
    core = lax.axis_index("core").reshape(1).astype(jnp.int32)
    partial = gram(core, own, other)
    plane = lax.all_to_all(partial.reshape(16, 128, 256), ("x", "y"), 0, 0, tiled=True)
    line = lax.all_to_all(sum_plane(plane), ("zh", "zl"), 0, 0, tiled=True)
    return sum_line(line)


def solution(mesh):
    fine = Mesh(mesh.devices.reshape(2, 4, 2, 4, 4), ("zh", "x", "core", "zl", "y"))
    rows, cells = ("zh", "x", "core"), ("zl", "y")
    return jax.shard_map(
        body,
        mesh=fine,
        in_specs=(
            P(rows, cells, None, None),
            P(),
            P(),
            P(),
            P(),
            P(cells, None),
            P(cells, None),
        ),
        out_specs=P(rows, cells),
        check_vma=False,
    )
```

time: 109 us -> 95.3 us (0.87)
  Pallas kernels: 19.9 us -> 14.2 us
  blocking collectives: 35.6 us -> 31.9 us
  waiting for transfers between devices: 32.1 us -> 29.4 us
  local copies, waits for them, and re-layouts: 5.3 us -> 3.83 us
    pallas_call x1, Pallas kernels: 4.55 us -> 1.4 us  [smooth_x_local(): pl.pallas_call(x_kernel, out_shape=jax.ShapeDtypeStruct((nx, columns, 512...]
    all_to_all x1, waiting for transfers between devices: 29.5 us -> 26.8 us  [body(): lax.all_to_all(sent.reshape(128, nz * ny // 128, width), ('zh', 'zl', 'x'...]
    all_to_all x1, blocking collectives: 22.6 us -> 20.5 us  [body(): lax.all_to_all(partial.reshape(16, 128, 256), ('x', 'y'), 0, 0, tiled=True)]
    pallas_call x1, Pallas kernels: 2.1 us -> 0.2 us  [sum_plane(): pl.pallas_call(sum_plane_kernel, out_shape=jax.ShapeDtypeStruct((8, 32, 1...]
    all_to_all x1, blocking collectives: 13.1 us -> 11.5 us  [body(): line = lax.all_to_all(sum_plane(plane), ('zh', 'zl'), 0, 0, tiled=True)]
    unnamed x14 -> x8, local copies, waits for them, and re-layouts: 5.3 us -> 3.83 us
    pallas_call x1 -> x2, Pallas kernels: 10.3 us -> 10.7 us  [the longest x1 8.69 us: smooth_zy(): pl.pallas_call(zy_kernel, out_shape=jax.ShapeDtypeStruct((nz, ny, slab *...]
  transfers between devices with their start and end apart: 2 -> 2, of which waited for: 2 -> 2; matrix products, arithmetic and copies ran while one was open for 0% -> 0% of each run, Pallas kernels for 0% -> 2%
where the time goes in v3:
time: 95.3 us; the launch traced here: 95 us
  blocking collectives  31.9 us (33%)
  waiting for transfers between devices  29.4 us (31%)
  starting transfers between devices  15.5 us (16%)
  Pallas kernels  14.2 us (15%)
  local copies, waits for them, and re-layouts  3.83 us (4%)
    all_to_all x1, waiting for transfers between devices, body(): lax.all_to_all(sent.reshape(128, nz * ny // 128, width), ('zh', 'zl', 'x'...  26.8 us
    all_to_all x1, blocking collectives, body(): lax.all_to_all(partial.reshape(16, 128, 256), ('x', 'y'), 0, 0, tiled=True)  20.5 us
    all_to_all x1, starting transfers between devices, body(): lax.all_to_all(sent.reshape(128, nz * ny // 128, width), ('zh', 'zl', 'x'...  15.4 us
    all_to_all x1, blocking collectives, body(): line = lax.all_to_all(sum_plane(plane), ('zh', 'zl'), 0, 0, tiled=True)  11.5 us
    pallas_call x1, Pallas kernels, smooth_zy(): pl.pallas_call(zy_kernel, out_shape=jax.ShapeDtypeStruct((nz, ny, slab *...  8.69 us
    unnamed x8, local copies, waits for them, and re-layouts  3.83 us
    ppermute x1, waiting for transfers between devices, body(): other = lax.ppermute(own, 'core', [(0, 1), (1, 0)])  2.64 us
    pallas_call x1, Pallas kernels, x_coefs(): pl.pallas_call(coef_kernel, out_shape=jax.ShapeDtypeStruct((nx, TAPS, 16,...  1.96 us
  transfers between devices with their start and end apart: 2, of which 2 were waited for; matrix products, arithmetic and copies ran while one was open for 0% of the time, Pallas kernels for 2%

profile of v3, /device:TPU:8, one launch (start us, length us, event | category | flops | bytes accessed | tf_op | source)
XLA Modules:
  0.0 95.0 jit_solution(967162083642674381)
XLA Ops:
  0.0 0.0 copy-start.3
  0.0 0.0 copy-start.2
  0.0 8.7 %smooth_zy.1 = bf16[32,64,256]{2,1,0:T(8,128)(2,1)} custom-call(f32[64,4,32,64]{3,2,1,0:T(8,128)} %bitcast.12, f32[4,64,64]{2,1,0:T(8,128)} %table_y.1, f32[4,32,32]{2,1,0:T(8,128)} %table_z.1, s32[4,32]{1,0:T(4,128)} %index_y.1, s32[4,64]{1,0:T(4,128)} %index_z.1), custom_call_target="tpu_custom_call" | custom-call | tf_op jit(solution)/shard_map/smooth_zy/pallas_call | solution.py:119
  8.7 15.4 %all-to-all-start = ((bf16[128,16,256]{2,1,0:T(8,128)(2,1)}), bf16[128,16,256]{2,1,0:T(8,128)(2,1)S(1)}, u32[]{:S(2)}, u32[]{:S(2)}) async-start(bf16[128,16,256]{2,1,0:T(8,128)(2,1)} %bitcast.13), calls=%async_computation | async-start | bytes 2097152 | tf_op jit(solution)/shard_map/all_to_all | solution.py:304
  24.1 0.1 pad_add_fusion.place
  24.2 0.0 copy-done.3
  24.2 0.0 copy-done.2
  24.2 2.0 %x_coefs.1.coef = f32[64,7,16,128]{3,2,1,0:T(8,128)S(1)} custom-call(s32[2]{0:T(128)S(1)} %pad_add_fusion.place, s32[32,64]{1,0:T(8,128)S(1)} %bitcast.11, f32[4,64,64]{2,1,0:T(8,128)S(1)} %copy-done.2), custom_call_target="tpu_custom_call" | custom-call | flops 4194304 | bytes 4194304 | tf_op jit(solution)/shard_map/x_coefs/pallas_call | solution.py:163
  26.1 0.0 copy-start
  26.1 1.8 %copy-done = f32[64,7,16,128]{3,2,1,0:T(8,128)} copy-done((f32[64,7,16,128]{3,2,1,0:T(8,128)}, f32[64,7,16,128]{3,2,1,0:T(8,128)S(1)}, u32[]{:S(2)}) %copy-start) | copy-done | bytes 3670040
  27.9 26.8 %all-to-all-done.got = bf16[128,16,256]{2,1,0:T(8,128)(2,1)S(1)} async-done(((bf16[128,16,256]{2,1,0:T(8,128)(2,1)}), bf16[128,16,256]{2,1,0:T(8,128)(2,1)S(1)}, u32[]{:S(2)}, u32[]{:S(2)}) %all-to-all-start) | async-done | bytes 1048608 | tf_op jit(solution)/shard_map/all_to_all | solution.py:304
  54.7 0.0 copy-start.1
  54.7 2.0 %copy-done.1 = f32[64,7,16,128]{3,2,1,0:T(8,128)S(1)} copy-done((f32[64,7,16,128]{3,2,1,0:T(8,128)S(1)}, f32[64,7,16,128]{3,2,1,0:T(8,128)}, u32[]{:S(2)}) %copy-start.1) | copy-done | bytes 3670040
  56.7 1.4 %smooth_x.1 = bf16[64,16,512]{2,1,0:T(8,128)(2,1)S(1)} custom-call(f32[64,7,16,128]{3,2,1,0:T(8,128)S(1)} %copy-done.1, bf16[128,16,256]{2,1,0:T(8,128)(2,1)S(1)} %all-to-all-done.got), custom_call_target="tpu_custom_call" | custom-call | tf_op jit(solution)/shard_map/smooth_x/pallas_call | solution.py:214
  58.1 0.1 collective-permute-start
  58.2 2.6 %collective-permute-done.other = bf16[1024,512]{1,0:T(8,128)(2,1)S(1)} collective-permute-done((bf16[1024,512]{1,0:T(8,128)(2,1)S(1)}, bf16[1024,512]{1,0:T(8,128)(2,1)S(1)}, u32[]{:S(2)}, u32[]{:S(2)}) %collective-permute-start) | collective-permute-done | bytes 1048608 | tf_op jit(solution)/shard_map/ppermute | solution.py:309
  60.9 1.3 %gram.1 = bf16[4,4,128,256]{3,2,1,0:T(8,128)(2,1)S(1)} custom-call(s32[1]{0:T(128)} %bitcast.core, bf16[1024,512]{1,0:T(8,128)(2,1)S(1)} %bitcast.10, bf16[1024,512]{1,0:T(8,128)(2,1)S(1)} %collective-permute-done.other), custom_call_target="tpu_custom_call" | custom-call | tf_op jit(solution)/shard_map/gram/pallas_call | solution.py:250
  62.2 20.5 %all_to_all.15.got = bf16[16,128,256]{2,1,0:T(8,128)(2,1)S(1)} all-to-all(bf16[16,128,256]{2,1,0:T(8,128)(2,1)S(1)} %bitcast.8), channel_id=1, replica_groups=mesh['zh'=2,'x'=4,'core'=2,'zl'=4,'y'=4] {'x','y'}, dimensions={0} | all-to-all | bytes 2097152 | tf_op jit(solution)/shard_map/all_to_all | solution.py:312
  82.7 0.2 sum_plane.1
  82.9 11.5 %all_to_all.16.got = f32[8,32,128]{2,1,0:T(8,128)S(1)} all-to-all(f32[8,32,128]{2,1,0:T(8,128)S(1)} %sum_plane.1), channel_id=1, replica_groups=mesh['zh'=2,'x'=4,'core'=2,'zl'=4,'y'=4] {'zh','zl'}, dimensions={0} | all-to-all | bytes 262144 | tf_op jit(solution)/shard_map/all_to_all | solution.py:313
  94.3 0.7 sum_line.1
Async XLA Ops:
  0.0 24.2 %copy-start.3 = (s32[64,32]{0,1:T(8,128)S(1)}, s32[64,32]{0,1:T(8,128)}, u32[]{:S(2)}) copy-start(s32[64,32]{0,1:T(8,128)} %param.11) | copy-start | bytes 24580
  0.0 24.2 %copy-start.2 = (f32[4,64,64]{2,1,0:T(8,128)S(1)}, f32[4,64,64]{2,1,0:T(8,128)}, u32[]{:S(2)}) copy-start(f32[4,64,64]{2,1,0:T(8,128)} %table_x.1) | copy-start | bytes 196612
  8.7 46.0 %all-to-all-start = ((bf16[128,16,256]{2,1,0:T(8,128)(2,1)}), bf16[128,16,256]{2,1,0:T(8,128)(2,1)S(1)}, u32[]{:S(2)}, u32[]{:S(2)}) async-start(bf16[128,16,256]{2,1,0:T(8,128)(2,1)} %bitcast.13), calls=%async_computation | async-start | bytes 2097152 | tf_op jit(solution)/shard_map/all_to_all | solution.py:304
  26.1 1.8 %copy-start = (f32[64,7,16,128]{3,2,1,0:T(8,128)}, f32[64,7,16,128]{3,2,1,0:T(8,128)S(1)}, u32[]{:S(2)}) copy-start(f32[64,7,16,128]{3,2,1,0:T(8,128)S(1)} %x_coefs.1.coef) | copy-start | bytes 11010052
  54.7 2.0 %copy-start.1 = (f32[64,7,16,128]{3,2,1,0:T(8,128)S(1)}, f32[64,7,16,128]{3,2,1,0:T(8,128)}, u32[]{:S(2)}) copy-start(f32[64,7,16,128]{3,2,1,0:T(8,128)} %copy-done) | copy-start | bytes 11010052
  58.1 2.7 %collective-permute-start = (bf16[1024,512]{1,0:T(8,128)(2,1)S(1)}, bf16[1024,512]{1,0:T(8,128)(2,1)S(1)}, u32[]{:S(2)}, u32[]{:S(2)}) collective-permute-start(bf16[1024,512]{1,0:T(8,128)(2,1)S(1)} %bitcast.9), channel_id=1, source_target_pairs={{0,16},{16,0},{1,17},{17,1},{2,18},{18,2},{3,19},{19,3},{4,20},{20... | collective-permute-start | bytes 3145736 | tf_op jit(solution)/shard_map/ppermute | solution.py:309

commit v4 on v3

--- a/solution.py
+++ b/solution.py
@@ -29,35 +29,39 @@
     return jnp.sum(jnp.where(cols == rows + (tap - BAND), table, 0.0), axis=1, keepdims=True)
 
 
-def zy_kernel(jac, table_y, table_z, index_y, index_z, out, planes, coef, lhs, ty, tz, iy, iz, sems, small):
-    slab, nz, rows, ny = planes.shape
+def zy_kernel(jac, table_y, table_z, index_y, index_z, out, planes, coef, lhs, done, ty, tz, iy, iz, sems, outs, small):
+    slab, _, rows, ny = planes.shape
+    nz = done.shape[0]
+    per = nz // GROUP
+    steps = slab // 2 * per
     loads = [
         pltpu.make_async_copy(s, d, small.at[k])
         for k, (s, d) in enumerate(((table_z, tz), (index_z, iz), (table_y, ty), (index_y, iy)))
     ]
     for load in loads:
         load.start()
-    waves = []
-    for x0 in range(0, slab, 2):
-        for w0 in range(0, nz, GROUP):
-            waves.append([(x, w) for w in range(w0, w0 + GROUP) for x in (x0, x0 + 1)])
-    copies = {}
-    started, waited = [0], [0]
-
-    def start_until(count):
-        while started[0] < min(count, len(waves)):
-            for x, w in waves[started[0]]:
-                copies[x, w] = pltpu.make_async_copy(jac.at[:, x, w, :], planes.at[x, w], sems.at[x, w])
-                copies[x, w].start()
-            started[0] += 1
-
-    def wait_until(count):
-        while waited[0] < min(count, len(waves)):
-            for x, w in waves[waited[0]]:
-                copies[x, w].wait()
-            waited[0] += 1
-
-    start_until(AHEAD)
+
+    def wave(step):
+        pair, group = step // per, step % per
+        for k in range(GROUP):
+            for x in range(2):
+                w = group * GROUP + k
+                yield pltpu.make_async_copy(
+                    jac.at[:, pair * 2 + x, w, :], planes.at[pair * 2 + x, w + BAND], sems.at[pair * 2 + x, w]
+                )
+
+    def result(step):
+        pair, group = step // per, step % per
+        place = (pl.ds(group * GROUP, GROUP), slice(None), pl.ds(pair * 2 * rows, 2 * rows))
+        return pltpu.make_async_copy(done.at[place], out.at[place], outs.at[step])
+
+    for step in range(AHEAD):
+        for copy in wave(step):
+            copy.start()
+    for x in range(slab):
+        for edge in range(BAND):
+            planes[x, edge] = jnp.zeros((rows, ny), F32)
+            planes[x, nz + BAND + edge] = jnp.zeros((rows, ny), F32)
     loads[0].wait()
     loads[1].wait()
     for tap in range(TAPS):
@@ -70,48 +74,53 @@
             coef[x, tap] = picked
     loads[2].wait()
     loads[3].wait()
+    split = [split_table(ty[t]) for t in range(TABLES)]
     for t in range(TABLES):
-        high, low = split_table(ty[t])
-        lhs[pl.ds(t * ny, ny), :] = jnp.concatenate([high, low], axis=1)
-    left = lhs[...]
-    lane = lax.broadcasted_iota(jnp.int32, (1, 2 * rows), 1)
+        for u in range(TABLES):
+            pieces = [split[t][0], split[u][0], split[t][1], split[u][1]]
+            lhs[t * TABLES + u] = jnp.concatenate(pieces, axis=1)
     half = rows // 2
-
-    def finish(both, z, x0):
-        for k, zz in enumerate((z, z + 1)):
-            label = jnp.where(lane < rows, iy[x0, zz], iy[x0 + 1, zz])
-            part = both[:, k * 2 * rows : (k + 1) * 2 * rows]
-            picked = part[:ny]
-            for t in range(1, TABLES):
-                picked = jnp.where(label == t, part[t * ny : (t + 1) * ny], picked)
-            out[zz, :, pl.ds(x0 * rows, 2 * rows)] = picked.astype(BF16)
-
-    pending = []
-    for x0 in range(0, slab, 2):
-        for z in range(0, nz, 2):
-            per = nz // GROUP
-            need = x0 // 2 * per + min(z + BAND + 1, nz - 1) // GROUP + 1
-            start_until(need + AHEAD - 1)
-            wait_until(need)
-            parts = {}
-            for x in (x0, x0 + 1):
-                for h in range(2):
-                    use = pl.ds(h * half, half)
-                    held = {w: planes[x, w, use, :] for w in range(max(z - BAND, 0), min(z + BAND + 2, nz))}
-                    for zz in (z, z + 1):
-                        total = None
-                        for w in range(max(zz - BAND, 0), min(zz + BAND + 1, nz)):
-                            term = coef[x, w - zz + BAND, pl.ds(zz, 1), :] * held[w]
-                            total = term if total is None else total + term
+    for copy in wave(0):
+        copy.wait()
+
+    for step in range(steps):
+        x0, group = step // per * 2, step % per
+
+        if step + AHEAD < steps:
+            for copy in wave(step + AHEAD):
+                copy.start()
+        if step + 1 < steps:
+            for copy in wave(step + 1):
+                copy.wait()
+
+        parts = {}
+        for x in range(2):
+            for h in range(2):
+                use = pl.ds(h * half, half)
+                for k0 in range(0, GROUP, 2):
+                    held = [planes[x0 + x, group * GROUP + k0 + j, use, :] for j in range(TAPS + 1)]
+                    for k in range(2):
+                        z = group * GROUP + k0 + k
+                        total = coef[x0 + x, 0, pl.ds(z, 1), :] * held[k]
+                        for tap in range(1, TAPS):
+                            total = total + coef[x0 + x, tap, pl.ds(z, 1), :] * held[k + tap]
                         short = total.astype(BF16)
-                        parts[zz, x, h] = jnp.concatenate([short, short], axis=1)
-            rhs = jnp.concatenate([parts[zz, x, h] for zz in (z, z + 1) for x in (x0, x0 + 1) for h in range(2)], axis=0)
-            both = lax.dot_general(left, rhs, (((1,), (1,)), ((), ())), preferred_element_type=F32)
-            pending.append((both, z, x0))
-            if len(pending) > 1:
-                finish(*pending.pop(0))
-    for item in pending:
-        finish(*item)
+                        blank = jnp.zeros_like(short)
+                        parts[k0 + k, x, h] = jnp.concatenate([blank, short] if x else [short, blank], axis=1)
+        for k in range(GROUP):
+            z = group * GROUP + k
+            rhs = jnp.concatenate([parts[k, x, h] for x in range(2) for h in range(2)], axis=0)
+            both = lax.dot_general(
+                lhs[iy[x0, z] * TABLES + iy[x0 + 1, z]],
+                jnp.concatenate([rhs, rhs], axis=1),
+                (((1,), (1,)), ((), ())),
+                preferred_element_type=F32,
+            )
+            done[z, :, pl.ds(x0 * rows, 2 * rows)] = both.astype(BF16)
+        result(step).start()
+
+    for step in range(steps):
+        result(step).wait()
 
 
 def smooth_zy(jacobian, smooth_y, smooth_z, index_y, index_z):
@@ -120,16 +129,18 @@
         zy_kernel,
         out_shape=jax.ShapeDtypeStruct((nz, ny, slab * rows), BF16),
         in_specs=[HBM] * 5,
-        out_specs=VMEM,
+        out_specs=HBM,
         scratch_shapes=[
-            pltpu.VMEM((slab, nz, rows, ny), F32),
+            pltpu.VMEM((slab, nz + 2 * BAND, rows, ny), F32),
             pltpu.VMEM((slab, TAPS, nz, ny), F32),
-            pltpu.VMEM((TABLES * ny, 2 * ny), BF16),
+            pltpu.VMEM((TABLES * TABLES, ny, 4 * ny), BF16),
+            pltpu.VMEM((nz, ny, slab * rows), BF16),
             pltpu.VMEM(smooth_y.shape, F32),
             pltpu.VMEM(smooth_z.shape, F32),
             pltpu.SMEM(index_y.shape, jnp.int32),
             pltpu.VMEM(index_z.shape, jnp.int32),
             pltpu.SemaphoreType.DMA((slab, nz)),
+            pltpu.SemaphoreType.DMA((slab // 2 * nz // GROUP,)),
             pltpu.SemaphoreType.DMA((4,)),
         ],
         compiler_params=pltpu.CompilerParams(vmem_limit_bytes=60 * 2**20),
@@ -139,9 +150,10 @@
 
 def coef_kernel(place, index_x, table_x, out, bands):
     z, y0 = place[0], place[1]
-    nx, taps, columns, lanes = out.shape
+    nx = table_x.shape[1]
+    _, columns, lanes = out.shape
     for t in range(TABLES):
-        for tap in range(taps):
+        for tap in range(TAPS):
             bands[t, tap] = jnp.broadcast_to(band_column(table_x[t], tap), (nx, lanes))
     row = index_x[pl.ds(z, 1), :]
     sub = lax.broadcasted_iota(jnp.int32, (columns, row.shape[1]), 0)
@@ -149,20 +161,26 @@
     label = jnp.sum(jnp.where(lan == sub + y0, row, 0).astype(F32), axis=1, keepdims=True)
     label = jnp.broadcast_to(label, (columns, lanes))
 
-    @pl.loop(0, nx)
-    def _(x):
-        for tap in range(taps):
-            picked = jnp.broadcast_to(bands[0, tap, pl.ds(x, 1), :], label.shape)
-            for t in range(1, TABLES):
-                picked = jnp.where(label == t, bands[t, tap, pl.ds(x, 1), :], picked)
-            out[x, tap] = picked
+    lane = lax.broadcasted_iota(jnp.int32, label.shape, 1)
+
+    @pl.loop(0, out.shape[0])
+    def _(cell):
+        total = jnp.zeros(label.shape, F32)
+        for k in range(4):
+            for tap in range(TAPS):
+                row = pl.ds(cell * 4 + k, 1)
+                picked = jnp.broadcast_to(bands[0, tap, row, :], label.shape)
+                for t in range(1, TABLES):
+                    picked = jnp.where(label == t, bands[t, tap, row, :], picked)
+                total = jnp.where(lane == k * TAPS + tap, picked, total)
+        out[cell] = total
 
 
 def x_coefs(place, index_x, smooth_x):
     nx = smooth_x.shape[1]
     return pl.pallas_call(
         coef_kernel,
-        out_shape=jax.ShapeDtypeStruct((nx, TAPS, 16, 128), F32),
+        out_shape=jax.ShapeDtypeStruct((nx // 4, 16, 128), F32),
         in_specs=[SMEM, VMEM, VMEM],
         out_specs=VMEM,
         scratch_shapes=[pltpu.VMEM((TABLES, TAPS, nx, 128), F32)],
@@ -183,34 +201,36 @@
         for parity in range(2):
             for zh in range(2):
                 first = zh * 64 + cell // 4 * 16 + parity * 4 + cell % 4
-                second = first + 8
                 use = pl.ds((parity * 2 + zh) * 128, 128)
                 for pair in range(2):
                     a = got[first, :, pl.ds(pair * 128, 128)].astype(F32)
-                    b = got[second, :, pl.ds(pair * 128, 128)].astype(F32)
+                    b = got[first + 8, :, pl.ds(pair * 128, 128)].astype(F32)
                     base = cell * 4 + pair * 2 + BAND
                     wide[base, :, use] = jnp.where(left, a, pltpu.roll(b, 64, 1))
                     wide[base + 1, :, use] = jnp.where(left, pltpu.roll(a, 64, 1), b)
         return carry
 
-    def smooth(step, carry):
-        x = step * 2
-        for block in range(lanes // 128):
-            use = pl.ds(block * 128, 128)
-            held = [wide[x + k, :, use] for k in range(TAPS + 1)]
-            for k in range(2):
-                total = coef[x + k, 0] * held[k]
-                for tap in range(1, TAPS):
-                    total = total + coef[x + k, tap] * held[k + tap]
-                out[x + k, :, use] = total.astype(BF16)
+    def smooth(cell, carry):
+        taps = coef[cell]
+        for k in range(4):
+            x = cell * 4 + k
+            totals = [None] * (lanes // 128)
+            for tap in range(TAPS):
+                column = k * TAPS + tap
+                factor = jnp.broadcast_to(taps[:, column : column + 1], (columns, 128))
+                for block in range(lanes // 128):
+                    term = factor * wide[x + tap, :, pl.ds(block * 128, 128)]
+                    totals[block] = term if tap == 0 else totals[block] + term
+            for block in range(lanes // 128):
+                out[x, :, pl.ds(block * 128, 128)] = totals[block].astype(BF16)
         return carry
 
     lax.fori_loop(0, nx // 4, merge, 0, unroll=16)
-    lax.fori_loop(0, nx // 2, smooth, 0, unroll=8)
+    lax.fori_loop(0, nx // 4, smooth, 0, unroll=16)
 
 
 def smooth_x_local(coef, got):
-    nx, _, columns, _ = coef.shape
+    nx, columns = coef.shape[0] * 4, coef.shape[1]
     return pl.pallas_call(
         x_kernel,
         out_shape=jax.ShapeDtypeStruct((nx, columns, 512), BF16),

time: 95.3 us -> 92.8 us (0.974)
  local copies, waits for them, and re-layouts: 3.83 us -> 0.01 us
  waiting for transfers between devices: 29.4 us -> 31.3 us
    unnamed x8 -> x4, local copies, waits for them, and re-layouts: 3.83 us -> 0.01 us
    all_to_all x1, waiting for transfers between devices: 26.8 us -> 28.6 us  [body(): lax.all_to_all(sent.reshape(128, nz * ny // 128, width), ('zh', 'zl', 'x'...]
    pallas_call x1, Pallas kernels: 8.69 us -> 7.49 us  [smooth_zy(): pl.pallas_call(zy_kernel, out_shape=jax.ShapeDtypeStruct((nz, ny, slab *...]
where the time goes in v4:
time: 92.8 us; the launch traced here: 92.4 us
  blocking collectives  31.9 us (34%)
  waiting for transfers between devices  31.3 us (34%)
  starting transfers between devices  15.4 us (17%)
  Pallas kernels  13.6 us (15%)
    all_to_all x1, waiting for transfers between devices, body(): lax.all_to_all(sent.reshape(128, nz * ny // 128, width), ('zh', 'zl', 'x'...  28.6 us
    all_to_all x1, blocking collectives, body(): lax.all_to_all(partial.reshape(16, 128, 256), ('x', 'y'), 0, 0, tiled=True)  20.5 us
    all_to_all x1, starting transfers between devices, body(): lax.all_to_all(sent.reshape(128, nz * ny // 128, width), ('zh', 'zl', 'x'...  15.4 us
    all_to_all x1, blocking collectives, body(): line = lax.all_to_all(sum_plane(plane), ('zh', 'zl'), 0, 0, tiled=True)  11.5 us
    pallas_call x1, Pallas kernels, smooth_zy(): pl.pallas_call(zy_kernel, out_shape=jax.ShapeDtypeStruct((nz, ny, slab *...  7.49 us
    ppermute x1, waiting for transfers between devices, body(): other = lax.ppermute(own, 'core', [(0, 1), (1, 0)])  2.64 us
    pallas_call x1, Pallas kernels, smooth_x_local(): pl.pallas_call(x_kernel, out_shape=jax.ShapeDtypeStruct((nx, columns, 512...  1.98 us
    pallas_call x1, Pallas kernels, x_coefs(): pl.pallas_call(coef_kernel, out_shape=jax.ShapeDtypeStruct((nx // 4, 16,...  1.91 us
  transfers between devices with their start and end apart: 2, of which 2 were waited for; matrix products, arithmetic and copies ran while one was open for 0% of the time, Pallas kernels for 2%

profile of v4, /device:TPU:8, one launch (start us, length us, event | category | flops | bytes accessed | tf_op | source)
XLA Modules:
  0.0 92.4 jit_solution(8492040035251088137)
XLA Ops:
  0.0 0.0 copy-start.1
  0.0 0.0 copy-start
  0.0 7.5 %smooth_zy.1 = bf16[32,64,256]{2,1,0:T(8,128)(2,1)} custom-call(f32[64,4,32,64]{3,2,1,0:T(8,128)} %bitcast.12, f32[4,64,64]{2,1,0:T(8,128)} %table_y.1, f32[4,32,32]{2,1,0:T(8,128)} %table_z.1, s32[4,32]{1,0:T(4,128)} %index_y.1, s32[4,64]{1,0:T(4,128)} %index_z.1), custom_call_target="tpu_custom_call" | custom-call | tf_op jit(solution)/shard_map/smooth_zy/pallas_call | solution.py:128
  7.5 15.4 %all-to-all-start = ((bf16[128,16,256]{2,1,0:T(8,128)(2,1)}), bf16[128,16,256]{2,1,0:T(8,128)(2,1)S(1)}, u32[]{:S(2)}, u32[]{:S(2)}) async-start(bf16[128,16,256]{2,1,0:T(8,128)(2,1)} %bitcast.13), calls=%async_computation | async-start | bytes 2097152 | tf_op jit(solution)/shard_map/all_to_all | solution.py:324
  22.9 0.1 pad_add_fusion.place
  23.0 0.0 copy-done.1
  23.0 0.0 copy-done
  23.0 1.9 %x_coefs.1.coef = f32[16,16,128]{2,1,0:T(8,128)S(1)} custom-call(s32[2]{0:T(128)S(1)} %pad_add_fusion.place, s32[32,64]{1,0:T(8,128)S(1)} %bitcast.11, f32[4,64,64]{2,1,0:T(8,128)S(1)} %copy-done), custom_call_target="tpu_custom_call" | custom-call | flops 4194304 | bytes 4194304 | tf_op jit(solution)/shard_map/x_coefs/pallas_call | solution.py:181
  24.9 28.6 %all-to-all-done.got = bf16[128,16,256]{2,1,0:T(8,128)(2,1)S(1)} async-done(((bf16[128,16,256]{2,1,0:T(8,128)(2,1)}), bf16[128,16,256]{2,1,0:T(8,128)(2,1)S(1)}, u32[]{:S(2)}, u32[]{:S(2)}) %all-to-all-start) | async-done | bytes 1048608 | tf_op jit(solution)/shard_map/all_to_all | solution.py:324
  53.5 2.0 %smooth_x.1 = bf16[64,16,512]{2,1,0:T(8,128)(2,1)S(1)} custom-call(f32[16,16,128]{2,1,0:T(8,128)S(1)} %x_coefs.1.coef, bf16[128,16,256]{2,1,0:T(8,128)(2,1)S(1)} %all-to-all-done.got), custom_call_target="tpu_custom_call" | custom-call | tf_op jit(solution)/shard_map/smooth_x/pallas_call | solution.py:234
  55.5 0.1 collective-permute-start
  55.6 2.6 %collective-permute-done.other = bf16[1024,512]{1,0:T(8,128)(2,1)S(1)} collective-permute-done((bf16[1024,512]{1,0:T(8,128)(2,1)S(1)}, bf16[1024,512]{1,0:T(8,128)(2,1)S(1)}, u32[]{:S(2)}, u32[]{:S(2)}) %collective-permute-start) | collective-permute-done | bytes 1048608 | tf_op jit(solution)/shard_map/ppermute | solution.py:329
  58.2 1.3 %gram.1 = bf16[4,4,128,256]{3,2,1,0:T(8,128)(2,1)S(1)} custom-call(s32[1]{0:T(128)} %bitcast.core, bf16[1024,512]{1,0:T(8,128)(2,1)S(1)} %bitcast.9, bf16[1024,512]{1,0:T(8,128)(2,1)S(1)} %collective-permute-done.other), custom_call_target="tpu_custom_call" | custom-call | tf_op jit(solution)/shard_map/gram/pallas_call | solution.py:270
  59.5 20.5 %all_to_all.15.got = bf16[16,128,256]{2,1,0:T(8,128)(2,1)S(1)} all-to-all(bf16[16,128,256]{2,1,0:T(8,128)(2,1)S(1)} %bitcast.10), channel_id=1, replica_groups=mesh['zh'=2,'x'=4,'core'=2,'zl'=4,'y'=4] {'x','y'}, dimensions={0} | all-to-all | bytes 2097152 | tf_op jit(solution)/shard_map/all_to_all | solution.py:332
  80.0 0.2 sum_plane.1
  80.2 11.5 %all_to_all.16.got = f32[8,32,128]{2,1,0:T(8,128)S(1)} all-to-all(f32[8,32,128]{2,1,0:T(8,128)S(1)} %sum_plane.1), channel_id=1, replica_groups=mesh['zh'=2,'x'=4,'core'=2,'zl'=4,'y'=4] {'zh','zl'}, dimensions={0} | all-to-all | bytes 262144 | tf_op jit(solution)/shard_map/all_to_all | solution.py:333
  91.7 0.7 sum_line.1
Async XLA Ops:
  0.0 23.0 %copy-start.1 = (s32[64,32]{0,1:T(8,128)S(1)}, s32[64,32]{0,1:T(8,128)}, u32[]{:S(2)}) copy-start(s32[64,32]{0,1:T(8,128)} %param.11) | copy-start | bytes 24580
  0.0 23.0 %copy-start = (f32[4,64,64]{2,1,0:T(8,128)S(1)}, f32[4,64,64]{2,1,0:T(8,128)}, u32[]{:S(2)}) copy-start(f32[4,64,64]{2,1,0:T(8,128)} %table_x.1) | copy-start | bytes 196612
  7.5 46.0 %all-to-all-start = ((bf16[128,16,256]{2,1,0:T(8,128)(2,1)}), bf16[128,16,256]{2,1,0:T(8,128)(2,1)S(1)}, u32[]{:S(2)}, u32[]{:S(2)}) async-start(bf16[128,16,256]{2,1,0:T(8,128)(2,1)} %bitcast.13), calls=%async_computation | async-start | bytes 2097152 | tf_op jit(solution)/shard_map/all_to_all | solution.py:324
  55.5 2.7 %collective-permute-start = (bf16[1024,512]{1,0:T(8,128)(2,1)S(1)}, bf16[1024,512]{1,0:T(8,128)(2,1)S(1)}, u32[]{:S(2)}, u32[]{:S(2)}) collective-permute-start(bf16[1024,512]{1,0:T(8,128)(2,1)S(1)} %bitcast.8), channel_id=1, source_target_pairs={{0,16},{16,0},{1,17},{17,1},{2,18},{18,2},{3,19},{19,3},{4,20},{20... | collective-permute-start | bytes 3145736 | tf_op jit(solution)/shard_map/ppermute | solution.py:329

commit v5 on v4

--- a/solution.py
+++ b/solution.py
@@ -1,3 +1,5 @@
+import functools
+
 import jax
 import jax.numpy as jnp
 from jax import lax
@@ -190,7 +192,7 @@
     )(place, jnp.swapaxes(index_x, 0, 1), smooth_x)
 
 
-def x_kernel(coef, got, out, wide):
+def x_kernel(parity, coef, got, out, wide):
     nx, columns, lanes = out.shape
     left = lax.broadcasted_iota(jnp.int32, (columns, 128), 1) < 64
     for edge in range(BAND):
@@ -198,16 +200,15 @@
         wide[nx + BAND + edge] = jnp.zeros(wide.shape[1:], F32)
 
     def merge(cell, carry):
-        for parity in range(2):
-            for zh in range(2):
-                first = zh * 64 + cell // 4 * 16 + parity * 4 + cell % 4
-                use = pl.ds((parity * 2 + zh) * 128, 128)
-                for pair in range(2):
-                    a = got[first, :, pl.ds(pair * 128, 128)].astype(F32)
-                    b = got[first + 8, :, pl.ds(pair * 128, 128)].astype(F32)
-                    base = cell * 4 + pair * 2 + BAND
-                    wide[base, :, use] = jnp.where(left, a, pltpu.roll(b, 64, 1))
-                    wide[base + 1, :, use] = jnp.where(left, pltpu.roll(a, 64, 1), b)
+        for zh in range(2):
+            first = zh * 64 + cell // 4 * 16 + parity * 4 + cell % 4
+            use = pl.ds(zh * 128, 128)
+            for pair in range(2):
+                a = got[first, :, pl.ds(pair * 128, 128)].astype(F32)
+                b = got[first + 8, :, pl.ds(pair * 128, 128)].astype(F32)
+                base = cell * 4 + pair * 2 + BAND
+                wide[base, :, use] = jnp.where(left, a, pltpu.roll(b, 64, 1))
+                wide[base + 1, :, use] = jnp.where(left, pltpu.roll(a, 64, 1), b)
         return carry
 
     def smooth(cell, carry):
@@ -229,14 +230,14 @@
     lax.fori_loop(0, nx // 4, smooth, 0, unroll=16)
 
 
-def smooth_x_local(coef, got):
+def smooth_x_local(parity, coef, got):
     nx, columns = coef.shape[0] * 4, coef.shape[1]
     return pl.pallas_call(
-        x_kernel,
-        out_shape=jax.ShapeDtypeStruct((nx, columns, 512), BF16),
+        functools.partial(x_kernel, parity),
+        out_shape=jax.ShapeDtypeStruct((nx, columns, 256), BF16),
         in_specs=[VMEM, VMEM],
         out_specs=VMEM,
-        scratch_shapes=[pltpu.VMEM((nx + 2 * BAND, columns, 512), F32)],
+        scratch_shapes=[pltpu.VMEM((nx + 2 * BAND, columns, 256), F32)],
         compiler_params=pltpu.CompilerParams(vmem_limit_bytes=12 * 2**20),
         name="smooth_x",
     )(coef, got)
@@ -248,33 +249,31 @@
     return parts[0]
 
 
-def gram_kernel(core, own, other, out):
-    mine = core[0]
-    left = own[...]
-    for k, right in enumerate((own, other)):
-        which = mine if k == 0 else 1 - mine
-        for part in range(2):
+def gram_kernel(core, even, odd, right_even, right_odd, *rest):
+    out = rest[-1]
+    which = core[0]
+    for x2, left in enumerate((even, odd)):
+        for y2, right in enumerate((right_even, right_odd)):
             piece = lax.dot_general(
-                left,
-                right[:, part * 256 : (part + 1) * 256],
-                (((0,), (0,)), ((), ())),
-                preferred_element_type=F32,
+                left[...], right[...], (((0,), (0,)), ((), ())), preferred_element_type=F32
             ).astype(BF16)
-            for x in range(4):
+            for x4 in range(2):
                 for zh in range(2):
-                    start = ((x % 2 * 2 + zh) * 2 + x // 2) * 64
-                    out[x, part * 2 + which, pl.ds(zh * 64, 64), :] = piece[start : start + 64]
-
-
-def gram(core, own, other):
+                    start = (zh * 2 + x4) * 64
+                    out[x4 * 2 + x2, y2 * 2 + which, pl.ds(zh * 64, 64), :] = piece[start : start + 64]
+
+
+def gram(core, left, right, *held):
     return pl.pallas_call(
         gram_kernel,
         out_shape=jax.ShapeDtypeStruct((4, 4, 128, 256), BF16),
-        in_specs=[SMEM, VMEM, VMEM],
-        out_specs=VMEM,
+        in_specs=[SMEM] + [VMEM] * (4 + len(held)),
+        out_specs=VMEM,
+        input_output_aliases={5: 0} if held else {},
         compiler_params=pltpu.CompilerParams(vmem_limit_bytes=16 * 2**20),
+        cost_estimate=pl.CostEstimate(flops=2**29, bytes_accessed=2**21, transcendentals=0),
         name="gram",
-    )(core, own, other)
+    )(core, *left, *right, *held)
 
 
 def sum_plane_kernel(got, out):
@@ -324,11 +323,12 @@
     got = lax.all_to_all(
         sent.reshape(128, nz * ny // 128, width), ("zh", "zl", "x", "y"), 0, 0, tiled=True
     )
-    panel = smooth_x_local(coef, got)
-    own = panel.reshape(-1, panel.shape[2])
-    other = lax.ppermute(own, "core", [(0, 1), (1, 0)])
     core = lax.axis_index("core").reshape(1).astype(jnp.int32)
-    partial = gram(core, own, other)
+    own, other = [], []
+    for parity in range(2):
+        own.append(smooth_x_local(parity, coef, got).reshape(-1, 256))
+        other.append(lax.ppermute(own[parity], "core", [(0, 1), (1, 0)]))
+    partial = gram(1 - core, own, other, gram(core, own, own))
     plane = lax.all_to_all(partial.reshape(16, 128, 256), ("x", "y"), 0, 0, tiled=True)
     line = lax.all_to_all(sum_plane(plane), ("zh", "zl"), 0, 0, tiled=True)
     return sum_line(line)

time: 92.8 us -> 93.5 us (level)
  waiting for transfers between devices: 31.3 us -> 29.4 us
  Pallas kernels: 13.6 us -> 15.2 us
    ppermute x1 -> x2, waiting for transfers between devices: 2.64 us -> 0.76 us  [body(): other.append(lax.ppermute(own[parity], 'core', [(0, 1), (1, 0)]))]
    pallas_call x1 -> x2, Pallas kernels: 1.98 us -> 3.43 us  [smooth_x_local(): pl.pallas_call(functools.partial(x_kernel, parity), out_shape=jax.ShapeDt...]
  transfers between devices with their start and end apart: 2 -> 3, of which waited for: 2 -> 2; matrix products, arithmetic and copies ran while one was open for 0% -> 0% of each run, Pallas kernels for 2% -> 5%
where the time goes in v5:
time: 93.5 us; the launch traced here: 93 us
  blocking collectives  32.2 us (34%)
  waiting for transfers between devices  29.4 us (31%)
  starting transfers between devices  16 us (17%)
  Pallas kernels  15.2 us (16%)
    all_to_all x1, waiting for transfers between devices, body(): lax.all_to_all(sent.reshape(128, nz * ny // 128, width), ('zh', 'zl', 'x'...  28.6 us
    all_to_all x1, blocking collectives, body(): lax.all_to_all(partial.reshape(16, 128, 256), ('x', 'y'), 0, 0, tiled=True)  20.7 us
    all_to_all x1, starting transfers between devices, body(): lax.all_to_all(sent.reshape(128, nz * ny // 128, width), ('zh', 'zl', 'x'...  15.4 us
    all_to_all x1, blocking collectives, body(): line = lax.all_to_all(sum_plane(plane), ('zh', 'zl'), 0, 0, tiled=True)  11.5 us
    pallas_call x1, Pallas kernels, smooth_zy(): pl.pallas_call(zy_kernel, out_shape=jax.ShapeDtypeStruct((nz, ny, slab *...  7.49 us
    pallas_call x2, Pallas kernels, smooth_x_local(): pl.pallas_call(functools.partial(x_kernel, parity), out_shape=jax.ShapeDt...  3.43 us
    pallas_call x1, Pallas kernels, x_coefs(): pl.pallas_call(coef_kernel, out_shape=jax.ShapeDtypeStruct((nx // 4, 16,...  1.91 us
  transfers between devices with their start and end apart: 3, of which 2 were waited for; matrix products, arithmetic and copies ran while one was open for 0% of the time, Pallas kernels for 5%

profile of v5, /device:TPU:8, one launch (start us, length us, event | category | flops | bytes accessed | tf_op | source)
XLA Modules:
  0.0 93.0 jit_solution(828120849647367400)
XLA Ops:
  0.0 0.0 copy-start.1
  0.0 0.0 copy-start
  0.0 7.5 %smooth_zy.1 = bf16[32,64,256]{2,1,0:T(8,128)(2,1)} custom-call(f32[64,4,32,64]{3,2,1,0:T(8,128)} %bitcast.19, f32[4,64,64]{2,1,0:T(8,128)} %table_y.1, f32[4,32,32]{2,1,0:T(8,128)} %table_z.1, s32[4,32]{1,0:T(4,128)} %index_y.1, s32[4,64]{1,0:T(4,128)} %index_z.1), custom_call_target="tpu_custom_call" | custom-call | tf_op jit(solution)/shard_map/smooth_zy/pallas_call | solution.py:130
  7.5 15.4 %all-to-all-start = ((bf16[128,16,256]{2,1,0:T(8,128)(2,1)}), bf16[128,16,256]{2,1,0:T(8,128)(2,1)S(1)}, u32[]{:S(2)}, u32[]{:S(2)}) async-start(bf16[128,16,256]{2,1,0:T(8,128)(2,1)} %bitcast.20), calls=%async_computation | async-start | bytes 2097152 | tf_op jit(solution)/shard_map/all_to_all | solution.py:323
  22.9 0.1 pad_add_fusion.place
  23.0 0.0 copy-done.1
  23.0 0.0 copy-done
  23.0 1.9 %x_coefs.1.coef = f32[16,16,128]{2,1,0:T(8,128)S(1)} custom-call(s32[2]{0:T(128)S(1)} %pad_add_fusion.place, s32[32,64]{1,0:T(8,128)S(1)} %bitcast.18, f32[4,64,64]{2,1,0:T(8,128)S(1)} %copy-done), custom_call_target="tpu_custom_call" | custom-call | flops 4194304 | bytes 4194304 | tf_op jit(solution)/shard_map/x_coefs/pallas_call | solution.py:183
  24.9 28.6 %all-to-all-done.got = bf16[128,16,256]{2,1,0:T(8,128)(2,1)S(1)} async-done(((bf16[128,16,256]{2,1,0:T(8,128)(2,1)}), bf16[128,16,256]{2,1,0:T(8,128)(2,1)S(1)}, u32[]{:S(2)}, u32[]{:S(2)}) %all-to-all-start) | async-done | bytes 1048608 | tf_op jit(solution)/shard_map/all_to_all | solution.py:323
  53.5 1.7 %smooth_x.3 = bf16[64,16,256]{2,1,0:T(8,128)(2,1)S(1)} custom-call(f32[16,16,128]{2,1,0:T(8,128)S(1)} %x_coefs.1.coef, bf16[128,16,256]{2,1,0:T(8,128)(2,1)S(1)} %all-to-all-done.got), custom_call_target="tpu_custom_call" | custom-call | tf_op jit(solution)/shard_map/smooth_x/pallas_call | solution.py:235
  55.2 0.1 collective-permute-start.1
  55.3 1.7 %smooth_x.2 = bf16[64,16,256]{2,1,0:T(8,128)(2,1)S(1)} custom-call(f32[16,16,128]{2,1,0:T(8,128)S(1)} %x_coefs.1.coef, bf16[128,16,256]{2,1,0:T(8,128)(2,1)S(1)} %all-to-all-done.got), custom_call_target="tpu_custom_call" | custom-call | tf_op jit(solution)/shard_map/smooth_x/pallas_call | solution.py:235
  57.0 0.6 collective-permute-start
  57.6 0.8 gram.2.rest_0_
  58.4 0.0 collective-permute-done.1.right_odd
  58.4 0.8 collective-permute-done.right_even
  59.2 0.8 gram.3
  59.9 20.7 %all_to_all.15.got = bf16[16,128,256]{2,1,0:T(8,128)(2,1)S(1)} all-to-all(bf16[16,128,256]{2,1,0:T(8,128)(2,1)S(1)} %bitcast.9), channel_id=1, replica_groups=mesh['zh'=2,'x'=4,'core'=2,'zl'=4,'y'=4] {'x','y'}, dimensions={0} | all-to-all | bytes 2097152 | tf_op jit(solution)/shard_map/all_to_all | solution.py:332
  80.6 0.2 sum_plane.1
  80.8 11.5 %all_to_all.16.got = f32[8,32,128]{2,1,0:T(8,128)S(1)} all-to-all(f32[8,32,128]{2,1,0:T(8,128)S(1)} %sum_plane.1), channel_id=1, replica_groups=mesh['zh'=2,'x'=4,'core'=2,'zl'=4,'y'=4] {'zh','zl'}, dimensions={0} | all-to-all | bytes 262144 | tf_op jit(solution)/shard_map/all_to_all | solution.py:333
  92.3 0.7 sum_line.1
Async XLA Ops:
  0.0 23.0 %copy-start.1 = (s32[64,32]{0,1:T(8,128)S(1)}, s32[64,32]{0,1:T(8,128)}, u32[]{:S(2)}) copy-start(s32[64,32]{0,1:T(8,128)} %param.11) | copy-start | bytes 24580
  0.0 23.0 %copy-start = (f32[4,64,64]{2,1,0:T(8,128)S(1)}, f32[4,64,64]{2,1,0:T(8,128)}, u32[]{:S(2)}) copy-start(f32[4,64,64]{2,1,0:T(8,128)} %table_x.1) | copy-start | bytes 196612
  7.5 46.0 %all-to-all-start = ((bf16[128,16,256]{2,1,0:T(8,128)(2,1)}), bf16[128,16,256]{2,1,0:T(8,128)(2,1)S(1)}, u32[]{:S(2)}, u32[]{:S(2)}) async-start(bf16[128,16,256]{2,1,0:T(8,128)(2,1)} %bitcast.20), calls=%async_computation | async-start | bytes 2097152 | tf_op jit(solution)/shard_map/all_to_all | solution.py:323
  55.2 3.2 %collective-permute-start.1 = (bf16[1024,256]{1,0:T(8,128)(2,1)S(1)}, bf16[1024,256]{1,0:T(8,128)(2,1)S(1)}, u32[]{:S(2)}, u32[]{:S(2)}) collective-permute-start(bf16[1024,256]{1,0:T(8,128)(2,1)S(1)} %bitcast.10), channel_id=1, source_target_pairs={{0,16},{16,0},{1,17},{17,1},{2,18},{18,2},{3,19},{19,3},{4,20},{20... | collective-permute-start | bytes 1572872 | tf_op jit(solution)/shard_map/ppermute | solution.py:330
  57.0 2.1 %collective-permute-start = (bf16[1024,256]{1,0:T(8,128)(2,1)S(1)}, bf16[1024,256]{1,0:T(8,128)(2,1)S(1)}, u32[]{:S(2)}, u32[]{:S(2)}) collective-permute-start(bf16[1024,256]{1,0:T(8,128)(2,1)S(1)} %bitcast.14), channel_id=1, source_target_pairs={{0,16},{16,0},{1,17},{17,1},{2,18},{18,2},{3,19},{19,3},{4,20},{20... | collective-permute-start | bytes 1572872 | tf_op jit(solution)/shard_map/ppermute | solution.py:330

commit v6 on v4

--- a/solution.py
+++ b/solution.py
@@ -47,13 +47,18 @@
             for x in range(2):
                 w = group * GROUP + k
                 yield pltpu.make_async_copy(
-                    jac.at[:, pair * 2 + x, w, :], planes.at[pair * 2 + x, w + BAND], sems.at[pair * 2 + x, w]
+                    jac.at[:, pair * 2 + x, w, :], planes.at[pair * 2 + x, w + BAND], sems.at[step]
                 )
+
+    def arrived(step):
+        pair, group = step // per, step % per
+        whole = planes.at[pl.ds(pair * 2, 2), pl.ds(group * GROUP + BAND, GROUP)]
+        pltpu.make_async_copy(whole, whole, sems.at[step]).wait()
 
     def result(step):
         pair, group = step // per, step % per
         place = (pl.ds(group * GROUP, GROUP), slice(None), pl.ds(pair * 2 * rows, 2 * rows))
-        return pltpu.make_async_copy(done.at[place], out.at[place], outs.at[step])
+        return pltpu.make_async_copy(done.at[place], out.at[place], outs)
 
     for step in range(AHEAD):
         for copy in wave(step):
@@ -80,8 +85,7 @@
             pieces = [split[t][0], split[u][0], split[t][1], split[u][1]]
             lhs[t * TABLES + u] = jnp.concatenate(pieces, axis=1)
     half = rows // 2
-    for copy in wave(0):
-        copy.wait()
+    arrived(0)
 
     for step in range(steps):
         x0, group = step // per * 2, step % per
@@ -90,8 +94,7 @@
             for copy in wave(step + AHEAD):
                 copy.start()
         if step + 1 < steps:
-            for copy in wave(step + 1):
-                copy.wait()
+            arrived(step + 1)
 
         parts = {}
         for x in range(2):
@@ -119,8 +122,7 @@
             done[z, :, pl.ds(x0 * rows, 2 * rows)] = both.astype(BF16)
         result(step).start()
 
-    for step in range(steps):
-        result(step).wait()
+    pltpu.make_async_copy(done, out, outs).wait()
 
 
 def smooth_zy(jacobian, smooth_y, smooth_z, index_y, index_z):
@@ -139,8 +141,8 @@
             pltpu.VMEM(smooth_z.shape, F32),
             pltpu.SMEM(index_y.shape, jnp.int32),
             pltpu.VMEM(index_z.shape, jnp.int32),
-            pltpu.SemaphoreType.DMA((slab, nz)),
             pltpu.SemaphoreType.DMA((slab // 2 * nz // GROUP,)),
+            pltpu.SemaphoreType.DMA,
             pltpu.SemaphoreType.DMA((4,)),
         ],
         compiler_params=pltpu.CompilerParams(vmem_limit_bytes=60 * 2**20),
@@ -248,33 +250,34 @@
     return parts[0]
 
 
-def gram_kernel(core, own, other, out):
-    mine = core[0]
+def gram_kernel(core, own, right, *rest):
+    out = rest[-1]
+    which = core[0]
     left = own[...]
-    for k, right in enumerate((own, other)):
-        which = mine if k == 0 else 1 - mine
-        for part in range(2):
-            piece = lax.dot_general(
-                left,
-                right[:, part * 256 : (part + 1) * 256],
-                (((0,), (0,)), ((), ())),
-                preferred_element_type=F32,
-            ).astype(BF16)
-            for x in range(4):
-                for zh in range(2):
-                    start = ((x % 2 * 2 + zh) * 2 + x // 2) * 64
-                    out[x, part * 2 + which, pl.ds(zh * 64, 64), :] = piece[start : start + 64]
-
-
-def gram(core, own, other):
+    for part in range(2):
+        piece = lax.dot_general(
+            left,
+            right[:, part * 256 : (part + 1) * 256],
+            (((0,), (0,)), ((), ())),
+            preferred_element_type=F32,
+        ).astype(BF16)
+        for x in range(4):
+            for zh in range(2):
+                start = ((x % 2 * 2 + zh) * 2 + x // 2) * 64
+                out[x, part * 2 + which, pl.ds(zh * 64, 64), :] = piece[start : start + 64]
+
+
+def gram(core, own, right, *held):
     return pl.pallas_call(
         gram_kernel,
         out_shape=jax.ShapeDtypeStruct((4, 4, 128, 256), BF16),
-        in_specs=[SMEM, VMEM, VMEM],
-        out_specs=VMEM,
+        in_specs=[SMEM] + [VMEM] * (2 + len(held)),
+        out_specs=VMEM,
+        input_output_aliases={3: 0} if held else {},
         compiler_params=pltpu.CompilerParams(vmem_limit_bytes=16 * 2**20),
+        cost_estimate=pl.CostEstimate(flops=2**29, bytes_accessed=2**21, transcendentals=0),
         name="gram",
-    )(core, own, other)
+    )(core, own, right, *held)
 
 
 def sum_plane_kernel(got, out):
@@ -328,7 +331,7 @@
     own = panel.reshape(-1, panel.shape[2])
     other = lax.ppermute(own, "core", [(0, 1), (1, 0)])
     core = lax.axis_index("core").reshape(1).astype(jnp.int32)
-    partial = gram(core, own, other)
+    partial = gram(1 - core, own, other, gram(core, own, own))
     plane = lax.all_to_all(partial.reshape(16, 128, 256), ("x", "y"), 0, 0, tiled=True)
     line = lax.all_to_all(sum_plane(plane), ("zh", "zl"), 0, 0, tiled=True)
     return sum_line(line)

time: 92.8 us -> 91.1 us (0.982)
  Pallas kernels: 13.6 us -> 12.5 us
    pallas_call x1, Pallas kernels: 7.49 us -> 6.28 us  [smooth_zy(): pl.pallas_call(zy_kernel, out_shape=jax.ShapeDtypeStruct((nz, ny, slab *...]
  transfers between devices with their start and end apart: 2 -> 2, of which waited for: 2 -> 2; matrix products, arithmetic and copies ran while one was open for 0% -> 0% of each run, Pallas kernels for 2% -> 3%
where the time goes in v6:
time: 91.1 us; the launch traced here: 90.6 us
  blocking collectives  31.9 us (35%)
  waiting for transfers between devices  30.5 us (33%)
  starting transfers between devices  15.4 us (17%)
  Pallas kernels  12.5 us (14%)
    all_to_all x1, waiting for transfers between devices, body(): lax.all_to_all(sent.reshape(128, nz * ny // 128, width), ('zh', 'zl', 'x'...  28.6 us
    all_to_all x1, blocking collectives, body(): lax.all_to_all(partial.reshape(16, 128, 256), ('x', 'y'), 0, 0, tiled=True)  20.5 us
    all_to_all x1, starting transfers between devices, body(): lax.all_to_all(sent.reshape(128, nz * ny // 128, width), ('zh', 'zl', 'x'...  15.4 us
    all_to_all x1, blocking collectives, body(): line = lax.all_to_all(sum_plane(plane), ('zh', 'zl'), 0, 0, tiled=True)  11.5 us
    pallas_call x1, Pallas kernels, smooth_zy(): pl.pallas_call(zy_kernel, out_shape=jax.ShapeDtypeStruct((nz, ny, slab *...  6.28 us
    pallas_call x1, Pallas kernels, smooth_x_local(): pl.pallas_call(x_kernel, out_shape=jax.ShapeDtypeStruct((nx, columns, 512...  1.98 us
    pallas_call x1, Pallas kernels, x_coefs(): pl.pallas_call(coef_kernel, out_shape=jax.ShapeDtypeStruct((nx // 4, 16,...  1.91 us
    ppermute x1, waiting for transfers between devices, body(): other = lax.ppermute(own, 'core', [(0, 1), (1, 0)])  1.91 us
  transfers between devices with their start and end apart: 2, of which 2 were waited for; matrix products, arithmetic and copies ran while one was open for 0% of the time, Pallas kernels for 3%

profile of v6, /device:TPU:8, one launch (start us, length us, event | category | flops | bytes accessed | tf_op | source)
XLA Modules:
  0.0 90.6 jit_solution(11462731506868658513)
XLA Ops:
  0.0 0.0 copy-start.1
  0.0 0.0 copy-start
  0.0 6.3 %smooth_zy.1 = bf16[32,64,256]{2,1,0:T(8,128)(2,1)} custom-call(f32[64,4,32,64]{3,2,1,0:T(8,128)} %bitcast.14, f32[4,64,64]{2,1,0:T(8,128)} %table_y.1, f32[4,32,32]{2,1,0:T(8,128)} %table_z.1, s32[4,32]{1,0:T(4,128)} %index_y.1, s32[4,64]{1,0:T(4,128)} %index_z.1), custom_call_target="tpu_custom_call" | custom-call | tf_op jit(solution)/shard_map/smooth_zy/pallas_call | solution.py:130
  6.3 15.4 %all-to-all-start = ((bf16[128,16,256]{2,1,0:T(8,128)(2,1)}), bf16[128,16,256]{2,1,0:T(8,128)(2,1)S(1)}, u32[]{:S(2)}, u32[]{:S(2)}) async-start(bf16[128,16,256]{2,1,0:T(8,128)(2,1)} %bitcast.15), calls=%async_computation | async-start | bytes 2097152 | tf_op jit(solution)/shard_map/all_to_all | solution.py:327
  21.7 0.1 pad_add_fusion.place
  21.7 0.0 copy-done.1
  21.7 0.0 copy-done
  21.8 1.9 %x_coefs.1.coef = f32[16,16,128]{2,1,0:T(8,128)S(1)} custom-call(s32[2]{0:T(128)S(1)} %pad_add_fusion.place, s32[32,64]{1,0:T(8,128)S(1)} %bitcast.13, f32[4,64,64]{2,1,0:T(8,128)S(1)} %copy-done), custom_call_target="tpu_custom_call" | custom-call | flops 4194304 | bytes 4194304 | tf_op jit(solution)/shard_map/x_coefs/pallas_call | solution.py:183
  23.7 28.6 %all-to-all-done.got = bf16[128,16,256]{2,1,0:T(8,128)(2,1)S(1)} async-done(((bf16[128,16,256]{2,1,0:T(8,128)(2,1)}), bf16[128,16,256]{2,1,0:T(8,128)(2,1)S(1)}, u32[]{:S(2)}, u32[]{:S(2)}) %all-to-all-start) | async-done | bytes 1048608 | tf_op jit(solution)/shard_map/all_to_all | solution.py:327
  52.3 2.0 %smooth_x.1 = bf16[64,16,512]{2,1,0:T(8,128)(2,1)S(1)} custom-call(f32[16,16,128]{2,1,0:T(8,128)S(1)} %x_coefs.1.coef, bf16[128,16,256]{2,1,0:T(8,128)(2,1)S(1)} %all-to-all-done.got), custom_call_target="tpu_custom_call" | custom-call | tf_op jit(solution)/shard_map/smooth_x/pallas_call | solution.py:236
  54.3 0.1 collective-permute-start
  54.4 0.7 gram.2.rest_0_
  55.1 1.9 %collective-permute-done.right = bf16[1024,512]{1,0:T(8,128)(2,1)S(1)} collective-permute-done((bf16[1024,512]{1,0:T(8,128)(2,1)S(1)}, bf16[1024,512]{1,0:T(8,128)(2,1)S(1)}, u32[]{:S(2)}, u32[]{:S(2)}) %collective-permute-start) | collective-permute-done | bytes 1048608 | tf_op jit(solution)/shard_map/ppermute | solution.py:332
  57.0 0.7 gram.3
  57.7 20.5 %all_to_all.15.got = bf16[16,128,256]{2,1,0:T(8,128)(2,1)S(1)} all-to-all(bf16[16,128,256]{2,1,0:T(8,128)(2,1)S(1)} %bitcast.12), channel_id=1, replica_groups=mesh['zh'=2,'x'=4,'core'=2,'zl'=4,'y'=4] {'x','y'}, dimensions={0} | all-to-all | bytes 2097152 | tf_op jit(solution)/shard_map/all_to_all | solution.py:335
  78.2 0.2 sum_plane.1
  78.4 11.5 %all_to_all.16.got = f32[8,32,128]{2,1,0:T(8,128)S(1)} all-to-all(f32[8,32,128]{2,1,0:T(8,128)S(1)} %sum_plane.1), channel_id=1, replica_groups=mesh['zh'=2,'x'=4,'core'=2,'zl'=4,'y'=4] {'zh','zl'}, dimensions={0} | all-to-all | bytes 262144 | tf_op jit(solution)/shard_map/all_to_all | solution.py:336
  89.9 0.7 sum_line.1
Async XLA Ops:
  0.0 21.7 %copy-start.1 = (s32[64,32]{0,1:T(8,128)S(1)}, s32[64,32]{0,1:T(8,128)}, u32[]{:S(2)}) copy-start(s32[64,32]{0,1:T(8,128)} %param.11) | copy-start | bytes 24580
  0.0 21.7 %copy-start = (f32[4,64,64]{2,1,0:T(8,128)S(1)}, f32[4,64,64]{2,1,0:T(8,128)}, u32[]{:S(2)}) copy-start(f32[4,64,64]{2,1,0:T(8,128)} %table_x.1) | copy-start | bytes 196612
  6.3 46.0 %all-to-all-start = ((bf16[128,16,256]{2,1,0:T(8,128)(2,1)}), bf16[128,16,256]{2,1,0:T(8,128)(2,1)S(1)}, u32[]{:S(2)}, u32[]{:S(2)}) async-start(bf16[128,16,256]{2,1,0:T(8,128)(2,1)} %bitcast.15), calls=%async_computation | async-start | bytes 2097152 | tf_op jit(solution)/shard_map/all_to_all | solution.py:327
  54.3 2.7 %collective-permute-start = (bf16[1024,512]{1,0:T(8,128)(2,1)S(1)}, bf16[1024,512]{1,0:T(8,128)(2,1)S(1)}, u32[]{:S(2)}, u32[]{:S(2)}) collective-permute-start(bf16[1024,512]{1,0:T(8,128)(2,1)S(1)} %bitcast.8), channel_id=1, source_target_pairs={{0,16},{16,0},{1,17},{17,1},{2,18},{18,2},{3,19},{19,3},{4,20},{20... | collective-permute-start | bytes 3145736 | tf_op jit(solution)/shard_map/ppermute | solution.py:332

commit v7 on v6

--- a/solution.py
+++ b/solution.py
@@ -1,3 +1,5 @@
+import functools
+
 import jax
 import jax.numpy as jnp
 from jax import lax
@@ -9,7 +11,7 @@
 TAPS = 2 * BAND + 1
 TABLES = 4
 GROUP = 8
-AHEAD = 3
+AHEAD = 4
 F32 = jnp.float32
 BF16 = jnp.bfloat16
 VMEM = pl.BlockSpec(memory_space=pltpu.VMEM)
@@ -61,8 +63,8 @@
         return pltpu.make_async_copy(done.at[place], out.at[place], outs)
 
     for step in range(AHEAD):
-        for copy in wave(step):
-            copy.start()
+        for k, copy in enumerate(wave(step)):
+            copy.start(priority=k % 2)
     for x in range(slab):
         for edge in range(BAND):
             planes[x, edge] = jnp.zeros((rows, ny), F32)
@@ -91,8 +93,8 @@
         x0, group = step // per * 2, step % per
 
         if step + AHEAD < steps:
-            for copy in wave(step + AHEAD):
-                copy.start()
+            for k, copy in enumerate(wave(step + AHEAD)):
+                copy.start(priority=k % 2)
         if step + 1 < steps:
             arrived(step + 1)
 
@@ -192,14 +194,15 @@
     )(place, jnp.swapaxes(index_x, 0, 1), smooth_x)
 
 
-def x_kernel(coef, got, out, wide):
+def x_kernel(part, coef, got, out, wide):
     nx, columns, lanes = out.shape
+    cells = nx // 4
     left = lax.broadcasted_iota(jnp.int32, (columns, 128), 1) < 64
-    for edge in range(BAND):
-        wide[edge] = jnp.zeros(wide.shape[1:], F32)
-        wide[nx + BAND + edge] = jnp.zeros(wide.shape[1:], F32)
-
-    def merge(cell, carry):
+    for edge in range(4):
+        wide[edge + part * (nx + 4)] = jnp.zeros(wide.shape[1:], F32)
+
+    for k in range(1 - part, cells + 2 - part):
+        cell = part * cells + k - 1
         for parity in range(2):
             for zh in range(2):
                 first = zh * 64 + cell // 4 * 16 + parity * 4 + cell % 4
@@ -207,41 +210,34 @@
                 for pair in range(2):
                     a = got[first, :, pl.ds(pair * 128, 128)].astype(F32)
                     b = got[first + 8, :, pl.ds(pair * 128, 128)].astype(F32)
-                    base = cell * 4 + pair * 2 + BAND
+                    base = k * 4 + pair * 2
                     wide[base, :, use] = jnp.where(left, a, pltpu.roll(b, 64, 1))
                     wide[base + 1, :, use] = jnp.where(left, pltpu.roll(a, 64, 1), b)
-        return carry
-
-    def smooth(cell, carry):
-        taps = coef[cell]
-        for k in range(4):
-            x = cell * 4 + k
-            totals = [None] * (lanes // 128)
-            for tap in range(TAPS):
-                column = k * TAPS + tap
-                factor = jnp.broadcast_to(taps[:, column : column + 1], (columns, 128))
-                for block in range(lanes // 128):
-                    term = factor * wide[x + tap, :, pl.ds(block * 128, 128)]
-                    totals[block] = term if tap == 0 else totals[block] + term
+
+    for x in range(nx):
+        taps = coef[part * cells + x // 4]
+        totals = [None] * (lanes // 128)
+        for tap in range(TAPS):
+            column = x % 4 * TAPS + tap
+            factor = jnp.broadcast_to(taps[:, column : column + 1], (columns, 128))
             for block in range(lanes // 128):
-                out[x, :, pl.ds(block * 128, 128)] = totals[block].astype(BF16)
-        return carry
-
-    lax.fori_loop(0, nx // 4, merge, 0, unroll=16)
-    lax.fori_loop(0, nx // 4, smooth, 0, unroll=16)
-
-
-def smooth_x_local(coef, got):
-    nx, columns = coef.shape[0] * 4, coef.shape[1]
-    return pl.pallas_call(
-        x_kernel,
+                term = factor * wide[x + tap + 4 - BAND, :, pl.ds(block * 128, 128)]
+                totals[block] = term if tap == 0 else totals[block] + term
+        for block in range(lanes // 128):
+            out[x, :, pl.ds(block * 128, 128)] = totals[block].astype(BF16)
+
+
+def smooth_x_local(part, coef, got):
+    nx, columns = coef.shape[0] * 2, coef.shape[1]
+    return pl.pallas_call(
+        functools.partial(x_kernel, part),
         out_shape=jax.ShapeDtypeStruct((nx, columns, 512), BF16),
         in_specs=[VMEM, VMEM],
         out_specs=VMEM,
-        scratch_shapes=[pltpu.VMEM((nx + 2 * BAND, columns, 512), F32)],
+        scratch_shapes=[pltpu.VMEM((nx + 8, columns, 512), F32)],
         compiler_params=pltpu.CompilerParams(vmem_limit_bytes=12 * 2**20),
         name="smooth_x",
-    )(coef, got)
+    )(coef, got).reshape(nx * columns, 512)
 
 
 def add_up(parts):
@@ -250,16 +246,18 @@
     return parts[0]
 
 
-def gram_kernel(core, own, right, *rest):
+def gram_kernel(core, own_a, own_b, right_a, right_b, *rest):
     out = rest[-1]
     which = core[0]
-    left = own[...]
     for part in range(2):
-        piece = lax.dot_general(
-            left,
-            right[:, part * 256 : (part + 1) * 256],
-            (((0,), (0,)), ((), ())),
-            preferred_element_type=F32,
+        piece = sum(
+            lax.dot_general(
+                own[...],
+                right[:, part * 256 : (part + 1) * 256],
+                (((0,), (0,)), ((), ())),
+                preferred_element_type=F32,
+            )
+            for own, right in ((own_a, right_a), (own_b, right_b))
         ).astype(BF16)
         for x in range(4):
             for zh in range(2):
@@ -271,13 +269,13 @@
     return pl.pallas_call(
         gram_kernel,
         out_shape=jax.ShapeDtypeStruct((4, 4, 128, 256), BF16),
-        in_specs=[SMEM] + [VMEM] * (2 + len(held)),
-        out_specs=VMEM,
-        input_output_aliases={3: 0} if held else {},
+        in_specs=[SMEM] + [VMEM] * (4 + len(held)),
+        out_specs=VMEM,
+        input_output_aliases={5: 0} if held else {},
         compiler_params=pltpu.CompilerParams(vmem_limit_bytes=16 * 2**20),
         cost_estimate=pl.CostEstimate(flops=2**29, bytes_accessed=2**21, transcendentals=0),
         name="gram",
-    )(core, own, right, *held)
+    )(core, *own, *right, *held)
 
 
 def sum_plane_kernel(got, out):
@@ -327,9 +325,10 @@
     got = lax.all_to_all(
         sent.reshape(128, nz * ny // 128, width), ("zh", "zl", "x", "y"), 0, 0, tiled=True
     )
-    panel = smooth_x_local(coef, got)
-    own = panel.reshape(-1, panel.shape[2])
-    other = lax.ppermute(own, "core", [(0, 1), (1, 0)])
+    own, other = [], []
+    for part in range(2):
+        own.append(smooth_x_local(part, coef, got))
+        other.append(lax.ppermute(own[part], "core", [(0, 1), (1, 0)]))
     core = lax.axis_index("core").reshape(1).astype(jnp.int32)
     partial = gram(1 - core, own, other, gram(core, own, own))
     plane = lax.all_to_all(partial.reshape(16, 128, 256), ("x", "y"), 0, 0, tiled=True)

time: 91.1 us -> 90.3 us (level)
  waiting for transfers between devices: 30.5 us -> 29.4 us
    ppermute x1 -> x2, waiting for transfers between devices: 1.91 us -> 0.77 us  [body(): other.append(lax.ppermute(own[part], 'core', [(0, 1), (1, 0)]))]
    pallas_call x1 -> x2, Pallas kernels: 1.98 us -> 2.06 us  [smooth_x_local(): pl.pallas_call(functools.partial(x_kernel, part), out_shape=jax.ShapeDtyp...]
  transfers between devices with their start and end apart: 2 -> 3, of which waited for: 2 -> 2; matrix products, arithmetic and copies ran while one was open for 0% -> 0% of each run, Pallas kernels for 3% -> 4%
where the time goes in v7:
time: 90.3 us; the launch traced here: 90 us
  blocking collectives  32.2 us (36%)
  waiting for transfers between devices  29.4 us (33%)
  starting transfers between devices  16 us (18%)
  Pallas kernels  12.3 us (14%)
    all_to_all x1, waiting for transfers between devices, body(): lax.all_to_all(sent.reshape(128, nz * ny // 128, width), ('zh', 'zl', 'x'...  28.6 us
    all_to_all x1, blocking collectives, body(): lax.all_to_all(partial.reshape(16, 128, 256), ('x', 'y'), 0, 0, tiled=True)  20.7 us
    all_to_all x1, starting transfers between devices, body(): lax.all_to_all(sent.reshape(128, nz * ny // 128, width), ('zh', 'zl', 'x'...  15.4 us
    all_to_all x1, blocking collectives, body(): line = lax.all_to_all(sum_plane(plane), ('zh', 'zl'), 0, 0, tiled=True)  11.5 us
    pallas_call x1, Pallas kernels, smooth_zy(): pl.pallas_call(zy_kernel, out_shape=jax.ShapeDtypeStruct((nz, ny, slab *...  5.91 us
    pallas_call x2, Pallas kernels, smooth_x_local(): pl.pallas_call(functools.partial(x_kernel, part), out_shape=jax.ShapeDtyp...  2.06 us
    pallas_call x1, Pallas kernels, x_coefs(): pl.pallas_call(coef_kernel, out_shape=jax.ShapeDtypeStruct((nx // 4, 16,...  1.91 us
  transfers between devices with their start and end apart: 3, of which 2 were waited for; matrix products, arithmetic and copies ran while one was open for 0% of the time, Pallas kernels for 4%

profile of v7, /device:TPU:8, one launch (start us, length us, event | category | flops | bytes accessed | tf_op | source)
XLA Modules:
  0.0 90.0 jit_solution(7743442545895653422)
XLA Ops:
  0.0 0.0 copy-start.1
  0.0 0.0 copy-start
  0.0 5.9 %smooth_zy.1 = bf16[32,64,256]{2,1,0:T(8,128)(2,1)} custom-call(f32[64,4,32,64]{3,2,1,0:T(8,128)} %bitcast.19, f32[4,64,64]{2,1,0:T(8,128)} %table_y.1, f32[4,32,32]{2,1,0:T(8,128)} %table_z.1, s32[4,32]{1,0:T(4,128)} %index_y.1, s32[4,64]{1,0:T(4,128)} %index_z.1), custom_call_target="tpu_custom_call" | custom-call | tf_op jit(solution)/shard_map/smooth_zy/pallas_call | solution.py:132
  5.9 15.4 %all-to-all-start = ((bf16[128,16,256]{2,1,0:T(8,128)(2,1)}), bf16[128,16,256]{2,1,0:T(8,128)(2,1)S(1)}, u32[]{:S(2)}, u32[]{:S(2)}) async-start(bf16[128,16,256]{2,1,0:T(8,128)(2,1)} %bitcast.20), calls=%async_computation | async-start | bytes 2097152 | tf_op jit(solution)/shard_map/all_to_all | solution.py:325
  21.3 0.1 pad_add_fusion.place
  21.4 0.0 copy-done.1
  21.4 0.0 copy-done
  21.4 1.9 %x_coefs.1.coef = f32[16,16,128]{2,1,0:T(8,128)S(1)} custom-call(s32[2]{0:T(128)S(1)} %pad_add_fusion.place, s32[32,64]{1,0:T(8,128)S(1)} %bitcast.18, f32[4,64,64]{2,1,0:T(8,128)S(1)} %copy-done), custom_call_target="tpu_custom_call" | custom-call | flops 4194304 | bytes 4194304 | tf_op jit(solution)/shard_map/x_coefs/pallas_call | solution.py:185
  23.3 28.6 %all-to-all-done.got = bf16[128,16,256]{2,1,0:T(8,128)(2,1)S(1)} async-done(((bf16[128,16,256]{2,1,0:T(8,128)(2,1)}), bf16[128,16,256]{2,1,0:T(8,128)(2,1)S(1)}, u32[]{:S(2)}, u32[]{:S(2)}) %all-to-all-start) | async-done | bytes 1048608 | tf_op jit(solution)/shard_map/all_to_all | solution.py:325
  51.9 1.0 %smooth_x.3 = bf16[32,16,512]{2,1,0:T(8,128)(2,1)S(1)} custom-call(f32[16,16,128]{2,1,0:T(8,128)S(1)} %x_coefs.1.coef, bf16[128,16,256]{2,1,0:T(8,128)(2,1)S(1)} %all-to-all-done.got), custom_call_target="tpu_custom_call" | custom-call | tf_op jit(solution)/shard_map/smooth_x/pallas_call | solution.py:232
  52.9 0.1 collective-permute-start.1
  53.0 1.0 %smooth_x.2 = bf16[32,16,512]{2,1,0:T(8,128)(2,1)S(1)} custom-call(f32[16,16,128]{2,1,0:T(8,128)S(1)} %x_coefs.1.coef, bf16[128,16,256]{2,1,0:T(8,128)(2,1)S(1)} %all-to-all-done.got), custom_call_target="tpu_custom_call" | custom-call | tf_op jit(solution)/shard_map/smooth_x/pallas_call | solution.py:232
  54.1 0.6 collective-permute-start
  54.7 0.8 gram.2.rest_0_
  55.4 0.0 collective-permute-done.1.right_b
  55.4 0.8 collective-permute-done.right_a
  56.2 0.8 gram.3
  57.0 20.7 %all_to_all.15.got = bf16[16,128,256]{2,1,0:T(8,128)(2,1)S(1)} all-to-all(bf16[16,128,256]{2,1,0:T(8,128)(2,1)S(1)} %bitcast.9), channel_id=1, replica_groups=mesh['zh'=2,'x'=4,'core'=2,'zl'=4,'y'=4] {'x','y'}, dimensions={0} | all-to-all | bytes 2097152 | tf_op jit(solution)/shard_map/all_to_all | solution.py:334
  77.7 0.2 sum_plane.1
  77.9 11.5 %all_to_all.16.got = f32[8,32,128]{2,1,0:T(8,128)S(1)} all-to-all(f32[8,32,128]{2,1,0:T(8,128)S(1)} %sum_plane.1), channel_id=1, replica_groups=mesh['zh'=2,'x'=4,'core'=2,'zl'=4,'y'=4] {'zh','zl'}, dimensions={0} | all-to-all | bytes 262144 | tf_op jit(solution)/shard_map/all_to_all | solution.py:335
  89.3 0.7 sum_line.1
Async XLA Ops:
  0.0 21.4 %copy-start.1 = (s32[64,32]{0,1:T(8,128)S(1)}, s32[64,32]{0,1:T(8,128)}, u32[]{:S(2)}) copy-start(s32[64,32]{0,1:T(8,128)} %param.11) | copy-start | bytes 24580
  0.0 21.4 %copy-start = (f32[4,64,64]{2,1,0:T(8,128)S(1)}, f32[4,64,64]{2,1,0:T(8,128)}, u32[]{:S(2)}) copy-start(f32[4,64,64]{2,1,0:T(8,128)} %table_x.1) | copy-start | bytes 196612
  5.9 46.0 %all-to-all-start = ((bf16[128,16,256]{2,1,0:T(8,128)(2,1)}), bf16[128,16,256]{2,1,0:T(8,128)(2,1)S(1)}, u32[]{:S(2)}, u32[]{:S(2)}) async-start(bf16[128,16,256]{2,1,0:T(8,128)(2,1)} %bitcast.20), calls=%async_computation | async-start | bytes 2097152 | tf_op jit(solution)/shard_map/all_to_all | solution.py:325
  52.9 2.5 %collective-permute-start.1 = (bf16[512,512]{1,0:T(8,128)(2,1)S(1)}, bf16[512,512]{1,0:T(8,128)(2,1)S(1)}, u32[]{:S(2)}, u32[]{:S(2)}) collective-permute-start(bf16[512,512]{1,0:T(8,128)(2,1)S(1)} %bitcast.10), channel_id=1, source_target_pairs={{0,16},{16,0},{1,17},{17,1},{2,18},{18,2},{3,19},{19,3},{4,20},{20... | collective-permute-start | bytes 1572872 | tf_op jit(solution)/shard_map/ppermute | solution.py:331
  54.1 2.1 %collective-permute-start = (bf16[512,512]{1,0:T(8,128)(2,1)S(1)}, bf16[512,512]{1,0:T(8,128)(2,1)S(1)}, u32[]{:S(2)}, u32[]{:S(2)}) collective-permute-start(bf16[512,512]{1,0:T(8,128)(2,1)S(1)} %bitcast.14), channel_id=1, source_target_pairs={{0,16},{16,0},{1,17},{17,1},{2,18},{18,2},{3,19},{19,3},{4,20},{20... | collective-permute-start | bytes 1572872 | tf_op jit(solution)/shard_map/ppermute | solution.py:331

commit v8 on v7

--- a/solution.py
+++ b/solution.py
@@ -10,8 +10,8 @@
 BAND = 3
 TAPS = 2 * BAND + 1
 TABLES = 4
-GROUP = 8
-AHEAD = 4
+GROUP = 16
+AHEAD = 2
 F32 = jnp.float32
 BF16 = jnp.bfloat16
 VMEM = pl.BlockSpec(memory_space=pltpu.VMEM)
@@ -95,14 +95,13 @@
         if step + AHEAD < steps:
             for k, copy in enumerate(wave(step + AHEAD)):
                 copy.start(priority=k % 2)
-        if step + 1 < steps:
-            arrived(step + 1)
-
         parts = {}
-        for x in range(2):
-            for h in range(2):
-                use = pl.ds(h * half, half)
-                for k0 in range(0, GROUP, 2):
+        for k0 in range(0, GROUP, 2):
+            if k0 + BAND + 1 in (GROUP, GROUP + 1) and step + 1 < steps:
+                arrived(step + 1)
+            for x in range(2):
+                for h in range(2):
+                    use = pl.ds(h * half, half)
                     held = [planes[x0 + x, group * GROUP + k0 + j, use, :] for j in range(TAPS + 1)]
                     for k in range(2):
                         z = group * GROUP + k0 + k
@@ -112,16 +111,16 @@
                         short = total.astype(BF16)
                         blank = jnp.zeros_like(short)
                         parts[k0 + k, x, h] = jnp.concatenate([blank, short] if x else [short, blank], axis=1)
-        for k in range(GROUP):
-            z = group * GROUP + k
-            rhs = jnp.concatenate([parts[k, x, h] for x in range(2) for h in range(2)], axis=0)
-            both = lax.dot_general(
-                lhs[iy[x0, z] * TABLES + iy[x0 + 1, z]],
-                jnp.concatenate([rhs, rhs], axis=1),
-                (((1,), (1,)), ((), ())),
-                preferred_element_type=F32,
-            )
-            done[z, :, pl.ds(x0 * rows, 2 * rows)] = both.astype(BF16)
+            for k in (k0, k0 + 1):
+                z = group * GROUP + k
+                rhs = jnp.concatenate([parts[k, x, h] for x in range(2) for h in range(2)], axis=0)
+                both = lax.dot_general(
+                    lhs[iy[x0, z] * TABLES + iy[x0 + 1, z]],
+                    jnp.concatenate([rhs, rhs], axis=1),
+                    (((1,), (1,)), ((), ())),
+                    preferred_element_type=F32,
+                )
+                done[z, :, pl.ds(x0 * rows, 2 * rows)] = both.astype(BF16)
         result(step).start()
 
     pltpu.make_async_copy(done, out, outs).wait()

time: 90.3 us -> 90 us (level)
  no operation moved by 1% of the time
where the time goes in v8:
time: 90 us; the launch traced here: 89.7 us
  blocking collectives  32.2 us (36%)
  waiting for transfers between devices  29.4 us (33%)
  starting transfers between devices  16 us (18%)
  Pallas kernels  11.9 us (13%)
    all_to_all x1, waiting for transfers between devices, body(): lax.all_to_all(sent.reshape(128, nz * ny // 128, width), ('zh', 'zl', 'x'...  28.6 us
    all_to_all x1, blocking collectives, body(): lax.all_to_all(partial.reshape(16, 128, 256), ('x', 'y'), 0, 0, tiled=True)  20.7 us
    all_to_all x1, starting transfers between devices, body(): lax.all_to_all(sent.reshape(128, nz * ny // 128, width), ('zh', 'zl', 'x'...  15.4 us
    all_to_all x1, blocking collectives, body(): line = lax.all_to_all(sum_plane(plane), ('zh', 'zl'), 0, 0, tiled=True)  11.5 us
    pallas_call x1, Pallas kernels, smooth_zy(): pl.pallas_call(zy_kernel, out_shape=jax.ShapeDtypeStruct((nz, ny, slab *...  5.57 us
    pallas_call x2, Pallas kernels, smooth_x_local(): pl.pallas_call(functools.partial(x_kernel, part), out_shape=jax.ShapeDtyp...  2.06 us
    pallas_call x1, Pallas kernels, x_coefs(): pl.pallas_call(coef_kernel, out_shape=jax.ShapeDtypeStruct((nx // 4, 16,...  1.91 us
  transfers between devices with their start and end apart: 3, of which 2 were waited for; matrix products, arithmetic and copies ran while one was open for 0% of the time, Pallas kernels for 4%

profile of v8, /device:TPU:8, one launch (start us, length us, event | category | flops | bytes accessed | tf_op | source)
XLA Modules:
  0.0 89.7 jit_solution(9187334005015366130)
XLA Ops:
  0.0 0.0 copy-start.1
  0.0 0.0 copy-start
  0.0 5.6 %smooth_zy.1 = bf16[32,64,256]{2,1,0:T(8,128)(2,1)} custom-call(f32[64,4,32,64]{3,2,1,0:T(8,128)} %bitcast.19, f32[4,64,64]{2,1,0:T(8,128)} %table_y.1, f32[4,32,32]{2,1,0:T(8,128)} %table_z.1, s32[4,32]{1,0:T(4,128)} %index_y.1, s32[4,64]{1,0:T(4,128)} %index_z.1), custom_call_target="tpu_custom_call" | custom-call | tf_op jit(solution)/shard_map/smooth_zy/pallas_call | solution.py:131
  5.6 15.4 %all-to-all-start = ((bf16[128,16,256]{2,1,0:T(8,128)(2,1)}), bf16[128,16,256]{2,1,0:T(8,128)(2,1)S(1)}, u32[]{:S(2)}, u32[]{:S(2)}) async-start(bf16[128,16,256]{2,1,0:T(8,128)(2,1)} %bitcast.20), calls=%async_computation | async-start | bytes 2097152 | tf_op jit(solution)/shard_map/all_to_all | solution.py:324
  20.9 0.1 pad_add_fusion.place
  21.0 0.0 copy-done.1
  21.0 0.0 copy-done
  21.0 1.9 %x_coefs.1.coef = f32[16,16,128]{2,1,0:T(8,128)S(1)} custom-call(s32[2]{0:T(128)S(1)} %pad_add_fusion.place, s32[32,64]{1,0:T(8,128)S(1)} %bitcast.18, f32[4,64,64]{2,1,0:T(8,128)S(1)} %copy-done), custom_call_target="tpu_custom_call" | custom-call | flops 4194304 | bytes 4194304 | tf_op jit(solution)/shard_map/x_coefs/pallas_call | solution.py:184
  22.9 28.6 %all-to-all-done.got = bf16[128,16,256]{2,1,0:T(8,128)(2,1)S(1)} async-done(((bf16[128,16,256]{2,1,0:T(8,128)(2,1)}), bf16[128,16,256]{2,1,0:T(8,128)(2,1)S(1)}, u32[]{:S(2)}, u32[]{:S(2)}) %all-to-all-start) | async-done | bytes 1048608 | tf_op jit(solution)/shard_map/all_to_all | solution.py:324
  51.6 1.0 %smooth_x.3 = bf16[32,16,512]{2,1,0:T(8,128)(2,1)S(1)} custom-call(f32[16,16,128]{2,1,0:T(8,128)S(1)} %x_coefs.1.coef, bf16[128,16,256]{2,1,0:T(8,128)(2,1)S(1)} %all-to-all-done.got), custom_call_target="tpu_custom_call" | custom-call | tf_op jit(solution)/shard_map/smooth_x/pallas_call | solution.py:231
  52.6 0.1 collective-permute-start.1
  52.7 1.0 %smooth_x.2 = bf16[32,16,512]{2,1,0:T(8,128)(2,1)S(1)} custom-call(f32[16,16,128]{2,1,0:T(8,128)S(1)} %x_coefs.1.coef, bf16[128,16,256]{2,1,0:T(8,128)(2,1)S(1)} %all-to-all-done.got), custom_call_target="tpu_custom_call" | custom-call | tf_op jit(solution)/shard_map/smooth_x/pallas_call | solution.py:231
  53.7 0.6 collective-permute-start
  54.3 0.8 gram.2.rest_0_
  55.1 0.0 collective-permute-done.1.right_b
  55.1 0.8 collective-permute-done.right_a
  55.9 0.8 gram.3
  56.6 20.7 %all_to_all.15.got = bf16[16,128,256]{2,1,0:T(8,128)(2,1)S(1)} all-to-all(bf16[16,128,256]{2,1,0:T(8,128)(2,1)S(1)} %bitcast.9), channel_id=1, replica_groups=mesh['zh'=2,'x'=4,'core'=2,'zl'=4,'y'=4] {'x','y'}, dimensions={0} | all-to-all | bytes 2097152 | tf_op jit(solution)/shard_map/all_to_all | solution.py:333
  77.3 0.2 sum_plane.1
  77.5 11.5 %all_to_all.16.got = f32[8,32,128]{2,1,0:T(8,128)S(1)} all-to-all(f32[8,32,128]{2,1,0:T(8,128)S(1)} %sum_plane.1), channel_id=1, replica_groups=mesh['zh'=2,'x'=4,'core'=2,'zl'=4,'y'=4] {'zh','zl'}, dimensions={0} | all-to-all | bytes 262144 | tf_op jit(solution)/shard_map/all_to_all | solution.py:334
  89.0 0.7 sum_line.1
Async XLA Ops:
  0.0 21.0 %copy-start.1 = (s32[64,32]{0,1:T(8,128)S(1)}, s32[64,32]{0,1:T(8,128)}, u32[]{:S(2)}) copy-start(s32[64,32]{0,1:T(8,128)} %param.11) | copy-start | bytes 24580
  0.0 21.0 %copy-start = (f32[4,64,64]{2,1,0:T(8,128)S(1)}, f32[4,64,64]{2,1,0:T(8,128)}, u32[]{:S(2)}) copy-start(f32[4,64,64]{2,1,0:T(8,128)} %table_x.1) | copy-start | bytes 196612
  5.6 46.0 %all-to-all-start = ((bf16[128,16,256]{2,1,0:T(8,128)(2,1)}), bf16[128,16,256]{2,1,0:T(8,128)(2,1)S(1)}, u32[]{:S(2)}, u32[]{:S(2)}) async-start(bf16[128,16,256]{2,1,0:T(8,128)(2,1)} %bitcast.20), calls=%async_computation | async-start | bytes 2097152 | tf_op jit(solution)/shard_map/all_to_all | solution.py:324
  52.6 2.5 %collective-permute-start.1 = (bf16[512,512]{1,0:T(8,128)(2,1)S(1)}, bf16[512,512]{1,0:T(8,128)(2,1)S(1)}, u32[]{:S(2)}, u32[]{:S(2)}) collective-permute-start(bf16[512,512]{1,0:T(8,128)(2,1)S(1)} %bitcast.10), channel_id=1, source_target_pairs={{0,16},{16,0},{1,17},{17,1},{2,18},{18,2},{3,19},{19,3},{4,20},{20... | collective-permute-start | bytes 1572872 | tf_op jit(solution)/shard_map/ppermute | solution.py:330
  53.7 2.1 %collective-permute-start = (bf16[512,512]{1,0:T(8,128)(2,1)S(1)}, bf16[512,512]{1,0:T(8,128)(2,1)S(1)}, u32[]{:S(2)}, u32[]{:S(2)}) collective-permute-start(bf16[512,512]{1,0:T(8,128)(2,1)S(1)} %bitcast.14), channel_id=1, source_target_pairs={{0,16},{16,0},{1,17},{17,1},{2,18},{18,2},{3,19},{19,3},{4,20},{20... | collective-permute-start | bytes 1572872 | tf_op jit(solution)/shard_map/ppermute | solution.py:330

commit v9 on v8

--- a/solution.py
+++ b/solution.py
@@ -11,7 +11,7 @@
 TAPS = 2 * BAND + 1
 TABLES = 4
 GROUP = 16
-AHEAD = 2
+AHEAD = 3
 F32 = jnp.float32
 BF16 = jnp.bfloat16
 VMEM = pl.BlockSpec(memory_space=pltpu.VMEM)
@@ -31,8 +31,9 @@
     return jnp.sum(jnp.where(cols == rows + (tap - BAND), table, 0.0), axis=1, keepdims=True)
 
 
-def zy_kernel(jac, table_y, table_z, index_y, index_z, out, planes, coef, lhs, done, ty, tz, iy, iz, sems, outs, small):
+def zy_kernel(jac, table_y, table_z, index_y, index_z, out, planes, merged, coef, lhs, done, ty, tz, iy, iz, sems, outs, small):
     slab, _, rows, ny = planes.shape
+    pairs = slab // 2
     nz = done.shape[0]
     per = nz // GROUP
     steps = slab // 2 * per
@@ -49,36 +50,41 @@
             for x in range(2):
                 w = group * GROUP + k
                 yield pltpu.make_async_copy(
-                    jac.at[:, pair * 2 + x, w, :], planes.at[pair * 2 + x, w + BAND], sems.at[step]
+                    jac.at[:, pair * 2 + x, w, :], planes.at[pair * 2 + x, w], sems.at[step]
                 )
 
     def arrived(step):
         pair, group = step // per, step % per
-        whole = planes.at[pl.ds(pair * 2, 2), pl.ds(group * GROUP + BAND, GROUP)]
+        whole = planes.at[pl.ds(pair * 2, 2), pl.ds(group * GROUP, GROUP)]
         pltpu.make_async_copy(whole, whole, sems.at[step]).wait()
+        for w in range(group * GROUP, (group + 1) * GROUP):
+            sides = [planes[pair * 2 + x, w] for x in range(2)]
+            merged[pair, w + BAND] = jnp.concatenate(sides, axis=1)
 
     def result(step):
         pair, group = step // per, step % per
         place = (pl.ds(group * GROUP, GROUP), slice(None), pl.ds(pair * 2 * rows, 2 * rows))
         return pltpu.make_async_copy(done.at[place], out.at[place], outs)
 
-    for step in range(AHEAD):
-        for k, copy in enumerate(wave(step)):
-            copy.start(priority=k % 2)
-    for x in range(slab):
+    for k, copy in enumerate(wave(0)):
+        copy.start(priority=k % 2)
+    for pair in range(pairs):
         for edge in range(BAND):
-            planes[x, edge] = jnp.zeros((rows, ny), F32)
-            planes[x, nz + BAND + edge] = jnp.zeros((rows, ny), F32)
+            merged[pair, edge] = jnp.zeros((rows, 2 * ny), F32)
+            merged[pair, nz + BAND + edge] = jnp.zeros((rows, 2 * ny), F32)
     loads[0].wait()
     loads[1].wait()
     for tap in range(TAPS):
         cols = [band_column(tz[t], tap) for t in range(TABLES)]
-        for x in range(slab):
-            label = iz[pl.ds(x, 1), :]
-            picked = jnp.broadcast_to(cols[0], (nz, ny))
+        for pair in range(pairs):
+            label = jnp.concatenate([iz[pl.ds(pair * 2 + x, 1), :] for x in range(2)], axis=1)
+            picked = jnp.broadcast_to(cols[0], (nz, 2 * ny))
             for t in range(1, TABLES):
                 picked = jnp.where(label == t, cols[t], picked)
-            coef[x, tap] = picked
+            coef[pair, tap] = picked
+    for step in range(1, AHEAD):
+        for k, copy in enumerate(wave(step)):
+            copy.start(priority=k % 2)
     loads[2].wait()
     loads[3].wait()
     split = [split_table(ty[t]) for t in range(TABLES)]
@@ -87,6 +93,7 @@
             pieces = [split[t][0], split[u][0], split[t][1], split[u][1]]
             lhs[t * TABLES + u] = jnp.concatenate(pieces, axis=1)
     half = rows // 2
+    first = lax.broadcasted_iota(jnp.int32, (half, 2 * ny), 1) < ny
     arrived(0)
 
     for step in range(steps):
@@ -99,18 +106,17 @@
         for k0 in range(0, GROUP, 2):
             if k0 + BAND + 1 in (GROUP, GROUP + 1) and step + 1 < steps:
                 arrived(step + 1)
-            for x in range(2):
-                for h in range(2):
-                    use = pl.ds(h * half, half)
-                    held = [planes[x0 + x, group * GROUP + k0 + j, use, :] for j in range(TAPS + 1)]
-                    for k in range(2):
-                        z = group * GROUP + k0 + k
-                        total = coef[x0 + x, 0, pl.ds(z, 1), :] * held[k]
-                        for tap in range(1, TAPS):
-                            total = total + coef[x0 + x, tap, pl.ds(z, 1), :] * held[k + tap]
-                        short = total.astype(BF16)
-                        blank = jnp.zeros_like(short)
-                        parts[k0 + k, x, h] = jnp.concatenate([blank, short] if x else [short, blank], axis=1)
+            for h in range(2):
+                use = pl.ds(h * half, half)
+                held = [merged[x0 // 2, group * GROUP + k0 + j, use, :] for j in range(TAPS + 1)]
+                for k in range(2):
+                    z = group * GROUP + k0 + k
+                    total = coef[x0 // 2, 0, pl.ds(z, 1), :] * held[k]
+                    for tap in range(1, TAPS):
+                        total = total + coef[x0 // 2, tap, pl.ds(z, 1), :] * held[k + tap]
+                    for x in range(2):
+                        side = jnp.where(first if x == 0 else ~first, total, 0.0)
+                        parts[k0 + k, x, h] = side.astype(BF16)
             for k in (k0, k0 + 1):
                 z = group * GROUP + k
                 rhs = jnp.concatenate([parts[k, x, h] for x in range(2) for h in range(2)], axis=0)
@@ -134,8 +140,9 @@
         in_specs=[HBM] * 5,
         out_specs=HBM,
         scratch_shapes=[
-            pltpu.VMEM((slab, nz + 2 * BAND, rows, ny), F32),
-            pltpu.VMEM((slab, TAPS, nz, ny), F32),
+            pltpu.VMEM((slab, nz, rows, ny), F32),
+            pltpu.VMEM((slab // 2, nz + 2 * BAND, rows, 2 * ny), F32),
+            pltpu.VMEM((slab // 2, TAPS, nz, 2 * ny), F32),
             pltpu.VMEM((TABLES * TABLES, ny, 4 * ny), BF16),
             pltpu.VMEM((nz, ny, slab * rows), BF16),
             pltpu.VMEM(smooth_y.shape, F32),

time: 90 us -> 89.9 us (level)
  no operation moved by 1% of the time
where the time goes in v9:
time: 89.9 us; the launch traced here: 89.5 us
  blocking collectives  32.2 us (36%)
  waiting for transfers between devices  29.4 us (33%)
  starting transfers between devices  16 us (18%)
  Pallas kernels  11.8 us (13%)
    all_to_all x1, waiting for transfers between devices, body(): lax.all_to_all(sent.reshape(128, nz * ny // 128, width), ('zh', 'zl', 'x'...  28.6 us
    all_to_all x1, blocking collectives, body(): lax.all_to_all(partial.reshape(16, 128, 256), ('x', 'y'), 0, 0, tiled=True)  20.7 us
    all_to_all x1, starting transfers between devices, body(): lax.all_to_all(sent.reshape(128, nz * ny // 128, width), ('zh', 'zl', 'x'...  15.4 us
    all_to_all x1, blocking collectives, body(): line = lax.all_to_all(sum_plane(plane), ('zh', 'zl'), 0, 0, tiled=True)  11.5 us
    pallas_call x1, Pallas kernels, smooth_zy(): pl.pallas_call(zy_kernel, out_shape=jax.ShapeDtypeStruct((nz, ny, slab *...  5.39 us
    pallas_call x2, Pallas kernels, smooth_x_local(): pl.pallas_call(functools.partial(x_kernel, part), out_shape=jax.ShapeDtyp...  2.06 us
    pallas_call x1, Pallas kernels, x_coefs(): pl.pallas_call(coef_kernel, out_shape=jax.ShapeDtypeStruct((nx // 4, 16,...  1.91 us
  transfers between devices with their start and end apart: 3, of which 2 were waited for; matrix products, arithmetic and copies ran while one was open for 0% of the time, Pallas kernels for 4%

profile of v9, /device:TPU:8, one launch (start us, length us, event | category | flops | bytes accessed | tf_op | source)
XLA Modules:
  0.0 89.5 jit_solution(18206207434012441834)
XLA Ops:
  0.0 0.0 copy-start.1
  0.0 0.0 copy-start
  0.0 5.4 %smooth_zy.1 = bf16[32,64,256]{2,1,0:T(8,128)(2,1)} custom-call(f32[64,4,32,64]{3,2,1,0:T(8,128)} %bitcast.19, f32[4,64,64]{2,1,0:T(8,128)} %table_y.1, f32[4,32,32]{2,1,0:T(8,128)} %table_z.1, s32[4,32]{1,0:T(4,128)} %index_y.1, s32[4,64]{1,0:T(4,128)} %index_z.1), custom_call_target="tpu_custom_call" | custom-call | tf_op jit(solution)/shard_map/smooth_zy/pallas_call | solution.py:137
  5.4 15.4 %all-to-all-start = ((bf16[128,16,256]{2,1,0:T(8,128)(2,1)}), bf16[128,16,256]{2,1,0:T(8,128)(2,1)S(1)}, u32[]{:S(2)}, u32[]{:S(2)}) async-start(bf16[128,16,256]{2,1,0:T(8,128)(2,1)} %bitcast.20), calls=%async_computation | async-start | bytes 2097152 | tf_op jit(solution)/shard_map/all_to_all | solution.py:331
  20.8 0.1 pad_add_fusion.place
  20.8 0.0 copy-done.1
  20.9 0.0 copy-done
  20.9 1.9 %x_coefs.1.coef = f32[16,16,128]{2,1,0:T(8,128)S(1)} custom-call(s32[2]{0:T(128)S(1)} %pad_add_fusion.place, s32[32,64]{1,0:T(8,128)S(1)} %bitcast.18, f32[4,64,64]{2,1,0:T(8,128)S(1)} %copy-done), custom_call_target="tpu_custom_call" | custom-call | flops 4194304 | bytes 4194304 | tf_op jit(solution)/shard_map/x_coefs/pallas_call | solution.py:191
  22.8 28.6 %all-to-all-done.got = bf16[128,16,256]{2,1,0:T(8,128)(2,1)S(1)} async-done(((bf16[128,16,256]{2,1,0:T(8,128)(2,1)}), bf16[128,16,256]{2,1,0:T(8,128)(2,1)S(1)}, u32[]{:S(2)}, u32[]{:S(2)}) %all-to-all-start) | async-done | bytes 1048608 | tf_op jit(solution)/shard_map/all_to_all | solution.py:331
  51.4 1.0 %smooth_x.3 = bf16[32,16,512]{2,1,0:T(8,128)(2,1)S(1)} custom-call(f32[16,16,128]{2,1,0:T(8,128)S(1)} %x_coefs.1.coef, bf16[128,16,256]{2,1,0:T(8,128)(2,1)S(1)} %all-to-all-done.got), custom_call_target="tpu_custom_call" | custom-call | tf_op jit(solution)/shard_map/smooth_x/pallas_call | solution.py:238
  52.4 0.1 collective-permute-start.1
  52.5 1.0 %smooth_x.2 = bf16[32,16,512]{2,1,0:T(8,128)(2,1)S(1)} custom-call(f32[16,16,128]{2,1,0:T(8,128)S(1)} %x_coefs.1.coef, bf16[128,16,256]{2,1,0:T(8,128)(2,1)S(1)} %all-to-all-done.got), custom_call_target="tpu_custom_call" | custom-call | tf_op jit(solution)/shard_map/smooth_x/pallas_call | solution.py:238
  53.6 0.6 collective-permute-start
  54.1 0.8 gram.2.rest_0_
  54.9 0.0 collective-permute-done.1.right_b
  54.9 0.8 collective-permute-done.right_a
  55.7 0.8 gram.3
  56.4 20.7 %all_to_all.15.got = bf16[16,128,256]{2,1,0:T(8,128)(2,1)S(1)} all-to-all(bf16[16,128,256]{2,1,0:T(8,128)(2,1)S(1)} %bitcast.9), channel_id=1, replica_groups=mesh['zh'=2,'x'=4,'core'=2,'zl'=4,'y'=4] {'x','y'}, dimensions={0} | all-to-all | bytes 2097152 | tf_op jit(solution)/shard_map/all_to_all | solution.py:340
  77.1 0.2 sum_plane.1
  77.4 11.5 %all_to_all.16.got = f32[8,32,128]{2,1,0:T(8,128)S(1)} all-to-all(f32[8,32,128]{2,1,0:T(8,128)S(1)} %sum_plane.1), channel_id=1, replica_groups=mesh['zh'=2,'x'=4,'core'=2,'zl'=4,'y'=4] {'zh','zl'}, dimensions={0} | all-to-all | bytes 262144 | tf_op jit(solution)/shard_map/all_to_all | solution.py:341
  88.8 0.7 sum_line.1
Async XLA Ops:
  0.0 20.9 %copy-start.1 = (s32[64,32]{0,1:T(8,128)S(1)}, s32[64,32]{0,1:T(8,128)}, u32[]{:S(2)}) copy-start(s32[64,32]{0,1:T(8,128)} %param.11) | copy-start | bytes 24580
  0.0 20.9 %copy-start = (f32[4,64,64]{2,1,0:T(8,128)S(1)}, f32[4,64,64]{2,1,0:T(8,128)}, u32[]{:S(2)}) copy-start(f32[4,64,64]{2,1,0:T(8,128)} %table_x.1) | copy-start | bytes 196612
  5.4 46.0 %all-to-all-start = ((bf16[128,16,256]{2,1,0:T(8,128)(2,1)}), bf16[128,16,256]{2,1,0:T(8,128)(2,1)S(1)}, u32[]{:S(2)}, u32[]{:S(2)}) async-start(bf16[128,16,256]{2,1,0:T(8,128)(2,1)} %bitcast.20), calls=%async_computation | async-start | bytes 2097152 | tf_op jit(solution)/shard_map/all_to_all | solution.py:331
  52.4 2.5 %collective-permute-start.1 = (bf16[512,512]{1,0:T(8,128)(2,1)S(1)}, bf16[512,512]{1,0:T(8,128)(2,1)S(1)}, u32[]{:S(2)}, u32[]{:S(2)}) collective-permute-start(bf16[512,512]{1,0:T(8,128)(2,1)S(1)} %bitcast.10), channel_id=1, source_target_pairs={{0,16},{16,0},{1,17},{17,1},{2,18},{18,2},{3,19},{19,3},{4,20},{20... | collective-permute-start | bytes 1572872 | tf_op jit(solution)/shard_map/ppermute | solution.py:337
  53.6 2.1 %collective-permute-start = (bf16[512,512]{1,0:T(8,128)(2,1)S(1)}, bf16[512,512]{1,0:T(8,128)(2,1)S(1)}, u32[]{:S(2)}, u32[]{:S(2)}) collective-permute-start(bf16[512,512]{1,0:T(8,128)(2,1)S(1)} %bitcast.14), channel_id=1, source_target_pairs={{0,16},{16,0},{1,17},{17,1},{2,18},{18,2},{3,19},{19,3},{4,20},{20... | collective-permute-start | bytes 1572872 | tf_op jit(solution)/shard_map/ppermute | solution.py:337

commit v10 on v9

--- a/solution.py
+++ b/solution.py
@@ -200,15 +200,17 @@
     )(place, jnp.swapaxes(index_x, 0, 1), smooth_x)
 
 
-def x_kernel(part, coef, got, out, wide):
+def x_kernel(start, coef, got, out, wide):
     nx, columns, lanes = out.shape
-    cells = nx // 4
+    count = nx // 4
     left = lax.broadcasted_iota(jnp.int32, (columns, 128), 1) < 64
-    for edge in range(4):
-        wide[edge + part * (nx + 4)] = jnp.zeros(wide.shape[1:], F32)
-
-    for k in range(1 - part, cells + 2 - part):
-        cell = part * cells + k - 1
+
+    for k in range(count + 2):
+        cell = start + k - 1
+        if not 0 <= cell < coef.shape[0]:
+            for x in range(4):
+                wide[k * 4 + x] = jnp.zeros(wide.shape[1:], F32)
+            continue
         for parity in range(2):
             for zh in range(2):
                 first = zh * 64 + cell // 4 * 16 + parity * 4 + cell % 4
@@ -221,7 +223,7 @@
                     wide[base + 1, :, use] = jnp.where(left, pltpu.roll(a, 64, 1), b)
 
     for x in range(nx):
-        taps = coef[part * cells + x // 4]
+        taps = coef[start + x // 4]
         totals = [None] * (lanes // 128)
         for tap in range(TAPS):
             column = x % 4 * TAPS + tap
@@ -233,10 +235,10 @@
             out[x, :, pl.ds(block * 128, 128)] = totals[block].astype(BF16)
 
 
-def smooth_x_local(part, coef, got):
-    nx, columns = coef.shape[0] * 2, coef.shape[1]
-    return pl.pallas_call(
-        functools.partial(x_kernel, part),
+def smooth_x_local(start, count, coef, got):
+    nx, columns = count * 4, coef.shape[1]
+    return pl.pallas_call(
+        functools.partial(x_kernel, start),
         out_shape=jax.ShapeDtypeStruct((nx, columns, 512), BF16),
         in_specs=[VMEM, VMEM],
         out_specs=VMEM,
@@ -252,36 +254,53 @@
     return parts[0]
 
 
-def gram_kernel(core, own_a, own_b, right_a, right_b, *rest):
-    out = rest[-1]
-    which = core[0]
+def product(lefts, rights, lanes):
+    return sum(
+        lax.dot_general(
+            left[...], right[:, lanes], (((0,), (0,)), ((), ())), preferred_element_type=F32
+        )
+        for left, right in zip(lefts, rights)
+    )
+
+
+def place_piece(out, part, which, piece):
+    piece = piece.astype(BF16)
+    for x in range(4):
+        for zh in range(2):
+            start = ((x % 2 * 2 + zh) * 2 + x // 2) * 64
+            out[x, part * 2 + which, pl.ds(zh * 64, 64), :] = piece[start : start + 64]
+
+
+def own_kernel(core, *refs):
+    *own, out = refs
     for part in range(2):
-        piece = sum(
-            lax.dot_general(
-                own[...],
-                right[:, part * 256 : (part + 1) * 256],
-                (((0,), (0,)), ((), ())),
-                preferred_element_type=F32,
-            )
-            for own, right in ((own_a, right_a), (own_b, right_b))
-        ).astype(BF16)
-        for x in range(4):
-            for zh in range(2):
-                start = ((x % 2 * 2 + zh) * 2 + x // 2) * 64
-                out[x, part * 2 + which, pl.ds(zh * 64, 64), :] = piece[start : start + 64]
-
-
-def gram(core, own, right, *held):
-    return pl.pallas_call(
-        gram_kernel,
-        out_shape=jax.ShapeDtypeStruct((4, 4, 128, 256), BF16),
-        in_specs=[SMEM] + [VMEM] * (4 + len(held)),
-        out_specs=VMEM,
-        input_output_aliases={5: 0} if held else {},
+        place_piece(out, part, core[0], product(own, own, slice(part * 256, (part + 1) * 256)))
+
+
+def early_kernel(left, right, out):
+    for part in range(2):
+        lanes = slice(part * 256, (part + 1) * 256)
+        out[:, lanes] = product((left,), (right,), lanes)
+
+
+def late_kernel(core, left, right, early, held, out):
+    for part in range(2):
+        lanes = slice(part * 256, (part + 1) * 256)
+        place_piece(out, part, core[0], early[:, lanes] + product((left,), (right,), lanes))
+
+
+def gram(kernel, shape, operands, aliases):
+    first = [SMEM] if operands[0].ndim == 1 else [VMEM]
+    return pl.pallas_call(
+        kernel,
+        out_shape=shape,
+        in_specs=first + [VMEM] * (len(operands) - 1),
+        out_specs=VMEM,
+        input_output_aliases=aliases,
         compiler_params=pltpu.CompilerParams(vmem_limit_bytes=16 * 2**20),
         cost_estimate=pl.CostEstimate(flops=2**29, bytes_accessed=2**21, transcendentals=0),
         name="gram",
-    )(core, *own, *right, *held)
+    )(*operands)
 
 
 def sum_plane_kernel(got, out):
@@ -332,11 +351,14 @@
         sent.reshape(128, nz * ny // 128, width), ("zh", "zl", "x", "y"), 0, 0, tiled=True
     )
     own, other = [], []
-    for part in range(2):
-        own.append(smooth_x_local(part, coef, got))
-        other.append(lax.ppermute(own[part], "core", [(0, 1), (1, 0)]))
+    for start, count in ((0, 8), (8, 8)):
+        own.append(smooth_x_local(start, count, coef, got))
+        other.append(lax.ppermute(own[-1], "core", [(0, 1), (1, 0)]))
     core = lax.axis_index("core").reshape(1).astype(jnp.int32)
-    partial = gram(1 - core, own, other, gram(core, own, own))
+    blocks = jax.ShapeDtypeStruct((4, 4, 128, 256), BF16)
+    held = gram(own_kernel, blocks, (core, *own), {})
+    early = gram(early_kernel, jax.ShapeDtypeStruct((512, 512), F32), (own[0], other[0]), {})
+    partial = gram(late_kernel, blocks, (1 - core, own[1], other[1], early, held), {4: 0})
     plane = lax.all_to_all(partial.reshape(16, 128, 256), ("x", "y"), 0, 0, tiled=True)
     line = lax.all_to_all(sum_plane(plane), ("zh", "zl"), 0, 0, tiled=True)
     return sum_line(line)

time: 89.9 us -> 89.6 us (level)
    pallas_call x4 -> x5, Pallas kernels: 3.57 us -> 3.79 us  [the longest x2 2.06 us: smooth_x_local(): pl.pallas_call(functools.partial(x_kernel, start), out_shape=jax.ShapeDty...]
  transfers between devices with their start and end apart: 3 -> 3, of which waited for: 2 -> 2; matrix products, arithmetic and copies ran while one was open for 0% -> 0% of each run, Pallas kernels for 4% -> 5%
where the time goes in v10:
time: 89.6 us; the launch traced here: 89.2 us
  blocking collectives  32.2 us (36%)
  waiting for transfers between devices  28.9 us (32%)
  starting transfers between devices  16 us (18%)
  Pallas kernels  12 us (13%)
    all_to_all x1, waiting for transfers between devices, body(): lax.all_to_all(sent.reshape(128, nz * ny // 128, width), ('zh', 'zl', 'x'...  28.6 us
    all_to_all x1, blocking collectives, body(): lax.all_to_all(partial.reshape(16, 128, 256), ('x', 'y'), 0, 0, tiled=True)  20.7 us
    all_to_all x1, starting transfers between devices, body(): lax.all_to_all(sent.reshape(128, nz * ny // 128, width), ('zh', 'zl', 'x'...  15.4 us
    all_to_all x1, blocking collectives, body(): line = lax.all_to_all(sum_plane(plane), ('zh', 'zl'), 0, 0, tiled=True)  11.5 us
    pallas_call x1, Pallas kernels, smooth_zy(): pl.pallas_call(zy_kernel, out_shape=jax.ShapeDtypeStruct((nz, ny, slab *...  5.39 us
    pallas_call x2, Pallas kernels, smooth_x_local(): pl.pallas_call(functools.partial(x_kernel, start), out_shape=jax.ShapeDty...  2.06 us
    pallas_call x1, Pallas kernels, x_coefs(): pl.pallas_call(coef_kernel, out_shape=jax.ShapeDtypeStruct((nx // 4, 16,...  1.91 us
  transfers between devices with their start and end apart: 3, of which 2 were waited for; matrix products, arithmetic and copies ran while one was open for 0% of the time, Pallas kernels for 5%

profile of v10, /device:TPU:8, one launch (start us, length us, event | category | flops | bytes accessed | tf_op | source)
XLA Modules:
  0.0 89.2 jit_solution(7750425745791488501)
XLA Ops:
  0.0 0.0 copy-start.1
  0.0 0.0 copy-start
  0.0 5.4 %smooth_zy.1 = bf16[32,64,256]{2,1,0:T(8,128)(2,1)} custom-call(f32[64,4,32,64]{3,2,1,0:T(8,128)} %bitcast.17, f32[4,64,64]{2,1,0:T(8,128)} %table_y.1, f32[4,32,32]{2,1,0:T(8,128)} %table_z.1, s32[4,32]{1,0:T(4,128)} %index_y.1, s32[4,64]{1,0:T(4,128)} %index_z.1), custom_call_target="tpu_custom_call" | custom-call | tf_op jit(solution)/shard_map/smooth_zy/pallas_call | solution.py:137
  5.4 15.4 %all-to-all-start = ((bf16[128,16,256]{2,1,0:T(8,128)(2,1)}), bf16[128,16,256]{2,1,0:T(8,128)(2,1)S(1)}, u32[]{:S(2)}, u32[]{:S(2)}) async-start(bf16[128,16,256]{2,1,0:T(8,128)(2,1)} %bitcast.18), calls=%async_computation | async-start | bytes 2097152 | tf_op jit(solution)/shard_map/all_to_all | solution.py:350
  20.8 0.1 pad_add_fusion.place
  20.8 0.0 copy-done.1
  20.9 0.0 copy-done
  20.9 1.9 %x_coefs.1.coef = f32[16,16,128]{2,1,0:T(8,128)S(1)} custom-call(s32[2]{0:T(128)S(1)} %pad_add_fusion.place, s32[32,64]{1,0:T(8,128)S(1)} %bitcast.16, f32[4,64,64]{2,1,0:T(8,128)S(1)} %copy-done), custom_call_target="tpu_custom_call" | custom-call | flops 4194304 | bytes 4194304 | tf_op jit(solution)/shard_map/x_coefs/pallas_call | solution.py:191
  22.8 28.6 %all-to-all-done.got = bf16[128,16,256]{2,1,0:T(8,128)(2,1)S(1)} async-done(((bf16[128,16,256]{2,1,0:T(8,128)(2,1)}), bf16[128,16,256]{2,1,0:T(8,128)(2,1)S(1)}, u32[]{:S(2)}, u32[]{:S(2)}) %all-to-all-start) | async-done | bytes 1048608 | tf_op jit(solution)/shard_map/all_to_all | solution.py:350
  51.4 1.0 %smooth_x.3 = bf16[32,16,512]{2,1,0:T(8,128)(2,1)S(1)} custom-call(f32[16,16,128]{2,1,0:T(8,128)S(1)} %x_coefs.1.coef, bf16[128,16,256]{2,1,0:T(8,128)(2,1)S(1)} %all-to-all-done.got), custom_call_target="tpu_custom_call" | custom-call | tf_op jit(solution)/shard_map/smooth_x/pallas_call | solution.py:240
  52.4 0.1 collective-permute-start.1
  52.5 1.0 %smooth_x.2 = bf16[32,16,512]{2,1,0:T(8,128)(2,1)S(1)} custom-call(f32[16,16,128]{2,1,0:T(8,128)S(1)} %x_coefs.1.coef, bf16[128,16,256]{2,1,0:T(8,128)(2,1)S(1)} %all-to-all-done.got), custom_call_target="tpu_custom_call" | custom-call | tf_op jit(solution)/shard_map/smooth_x/pallas_call | solution.py:240
  53.6 0.6 collective-permute-start
  54.1 0.8 gram.4.held
  54.9 0.0 collective-permute-done.1.right
  54.9 0.5 gram.3.early
  55.4 0.3 collective-permute-done.right
  55.7 0.5 gram.5
  56.2 20.7 %all_to_all.15.got = bf16[16,128,256]{2,1,0:T(8,128)(2,1)S(1)} all-to-all(bf16[16,128,256]{2,1,0:T(8,128)(2,1)S(1)} %bitcast.9), channel_id=1, replica_groups=mesh['zh'=2,'x'=4,'core'=2,'zl'=4,'y'=4] {'x','y'}, dimensions={0} | all-to-all | bytes 2097152 | tf_op jit(solution)/shard_map/all_to_all | solution.py:362
  76.9 0.2 sum_plane.1
  77.1 11.5 %all_to_all.16.got = f32[8,32,128]{2,1,0:T(8,128)S(1)} all-to-all(f32[8,32,128]{2,1,0:T(8,128)S(1)} %sum_plane.1), channel_id=1, replica_groups=mesh['zh'=2,'x'=4,'core'=2,'zl'=4,'y'=4] {'zh','zl'}, dimensions={0} | all-to-all | bytes 262144 | tf_op jit(solution)/shard_map/all_to_all | solution.py:363
  88.5 0.7 sum_line.1
Async XLA Ops:
  0.0 20.9 %copy-start.1 = (s32[64,32]{0,1:T(8,128)S(1)}, s32[64,32]{0,1:T(8,128)}, u32[]{:S(2)}) copy-start(s32[64,32]{0,1:T(8,128)} %param.11) | copy-start | bytes 24580
  0.0 20.9 %copy-start = (f32[4,64,64]{2,1,0:T(8,128)S(1)}, f32[4,64,64]{2,1,0:T(8,128)}, u32[]{:S(2)}) copy-start(f32[4,64,64]{2,1,0:T(8,128)} %table_x.1) | copy-start | bytes 196612
  5.4 46.0 %all-to-all-start = ((bf16[128,16,256]{2,1,0:T(8,128)(2,1)}), bf16[128,16,256]{2,1,0:T(8,128)(2,1)S(1)}, u32[]{:S(2)}, u32[]{:S(2)}) async-start(bf16[128,16,256]{2,1,0:T(8,128)(2,1)} %bitcast.18), calls=%async_computation | async-start | bytes 2097152 | tf_op jit(solution)/shard_map/all_to_all | solution.py:350
  52.4 2.5 %collective-permute-start.1 = (bf16[512,512]{1,0:T(8,128)(2,1)S(1)}, bf16[512,512]{1,0:T(8,128)(2,1)S(1)}, u32[]{:S(2)}, u32[]{:S(2)}) collective-permute-start(bf16[512,512]{1,0:T(8,128)(2,1)S(1)} %bitcast.13), channel_id=1, source_target_pairs={{0,16},{16,0},{1,17},{17,1},{2,18},{18,2},{3,19},{19,3},{4,20},{20... | collective-permute-start | bytes 1572872 | tf_op jit(solution)/shard_map/ppermute | solution.py:356
  53.6 2.1 %collective-permute-start = (bf16[512,512]{1,0:T(8,128)(2,1)S(1)}, bf16[512,512]{1,0:T(8,128)(2,1)S(1)}, u32[]{:S(2)}, u32[]{:S(2)}) collective-permute-start(bf16[512,512]{1,0:T(8,128)(2,1)S(1)} %bitcast.10), channel_id=1, source_target_pairs={{0,16},{16,0},{1,17},{17,1},{2,18},{18,2},{3,19},{19,3},{4,20},{20... | collective-permute-start | bytes 1572872 | tf_op jit(solution)/shard_map/ppermute | solution.py:356
